TPU v7x, 512 devices: a whole 4x4x16 slice. The times are simulated.
512 devices in a mesh: dp: 128 (over y, z, core), sp: 4 (over x).
Axes of the slice: x: 4, y: 4, z: 16, core: 2. Of those that a mesh axis runs over, the one named last changes fastest.
Arguments:
- queries: bfloat16 [65536, 3584], P(('dp', 'sp')), may hold values from -128 to 128
- keys: bfloat16 [65536, 512], P(('dp', 'sp')), may hold values from -6 to 6
- values: bfloat16 [65536, 512], P(('dp', 'sp')), may hold values from -6 to 6
- document_lengths: int32 [128, 8], P('dp'), may hold values from 1 to 256, 512 in all within a row
- pair_ids: int32 [1024], P('dp'), may hold values from 0 to 1023, as said below
Outputs:
- embeddings: bfloat16 [1024, 3584], P('dp', 'sp')
- grads: float32 [1024, 3584], P('dp', 'sp')
Inputs may be any that keep to these rules, and one draw needn't show every extreme that they name: `document_lengths`: each row's 8 lengths sum to 512; the longest is exactly 256. pair_ids pairs the 1024 documents two by two: pair_ids[pair_ids[i]] = i and pair_ids[i] != i.
All inputs are finite; a program needn't handle non-finite values.
Results may differ from a plain program's by a relative error of at most 0.0055.
Values may be sent and summed in bfloat16 or wider, within the bound.
A program may use at most 64 MiB of HBM per device.

v0:
```python
import math

import jax
import jax.numpy as jnp
from jax import lax
from jax.sharding import PartitionSpec as P

QUERY_HEADS = 28
KEY_VALUE_HEADS = 4
HEAD_SIZE = 128
DOCS = 8


SOFTMAX_TEMP = 0.02


def segment_of(lengths, count):
    ends = jnp.cumsum(lengths)
    places = jnp.arange(count, dtype=jnp.int32)
    return jnp.sum((places[:, None] >= ends[None, :]).astype(jnp.int32), axis=1)


def attend(query_flat, row_segment, key_head, value_head, segment):
    total = query_flat.shape[0]
    block_rows = math.gcd(total, 512)
    query_blocks = query_flat.reshape(total // block_rows, block_rows, query_flat.shape[1])
    segment_blocks = row_segment.reshape(total // block_rows, block_rows)

    def one_block(inputs):
        query_block, segment_block = inputs
        scores = lax.dot_general(
            query_block, key_head, (((1,), (1,)), ((), ())), preferred_element_type=jnp.float32
        ) * HEAD_SIZE ** (-0.5)
        scores = jnp.where(segment_block[:, None] == segment[None, :], scores, -jnp.inf)
        largest = jnp.max(scores, axis=1, keepdims=True)
        weights = jnp.exp(scores - largest)
        probs = (weights / jnp.sum(weights, axis=1, keepdims=True)).astype(jnp.bfloat16)
        return jnp.dot(probs, value_head, preferred_element_type=jnp.float32).astype(jnp.bfloat16)

    return lax.map(one_block, (query_blocks, segment_blocks)).reshape(total, value_head.shape[1])


def per_device(queries, keys, values, document_lengths, pair_ids):
    lengths = document_lengths[0]
    parts = lax.axis_size("sp")
    tokens_here = queries.shape[0]
    seq_len = tokens_here * parts
    segment = segment_of(lengths, seq_len)
    head_group = QUERY_HEADS // KEY_VALUE_HEADS
    doc_index = jnp.arange(DOCS, dtype=jnp.int32)
    stacked = jnp.stack([keys, values])
    query_rows, kv_rows = (
        lax.all_to_all(queries[None], "sp", split_axis=2, concat_axis=1, tiled=True),
        lax.all_to_all(stacked, "sp", split_axis=2, concat_axis=1, tiled=True),
    )
    flat = query_rows[0].reshape(seq_len * head_group, HEAD_SIZE)
    result = attend(flat, jnp.repeat(segment, head_group), kv_rows[0], kv_rows[1], segment)
    attended = result.reshape(seq_len, head_group * HEAD_SIZE)
    onehot = (segment[None, :] == doc_index[:, None]).astype(jnp.bfloat16)
    summed = jnp.dot(onehot, attended, preferred_element_type=jnp.float32)
    pooled = summed / lengths[:, None].astype(jnp.float32)
    squares = lax.psum(jnp.sum(pooled * pooled, axis=1), "sp")
    radius = jnp.sqrt(squares + 1e-06)[:, None]
    embeddings = (pooled / radius).astype(jnp.bfloat16)
    every = lax.all_gather(embeddings, "dp", axis=0, tiled=True)
    partial_scores = lax.dot_general(
        embeddings, every, (((1,), (1,)), ((), ())), preferred_element_type=jnp.float32
    )
    score_logits = lax.psum(partial_scores, "sp") / SOFTMAX_TEMP
    columns = jnp.arange(every.shape[0], dtype=jnp.int32)
    own_rows = lax.axis_index("dp") * DOCS + doc_index
    score_logits = jnp.where(own_rows[:, None] == columns[None, :], -jnp.inf, score_logits)
    largest = jnp.max(score_logits, axis=1, keepdims=True)
    weights = jnp.exp(score_logits - largest)
    probs = weights / jnp.sum(weights, axis=1, keepdims=True)
    loss_coefficient = probs - (columns[None, :] == pair_ids[:, None]).astype(jnp.float32)
    every_wide = every.astype(jnp.float32)
    own_wide = embeddings.astype(jnp.float32)
    row_piece = jnp.dot(loss_coefficient, every_wide, precision=lax.Precision.HIGHEST)
    column_piece = lax.psum_scatter(
        jnp.dot(loss_coefficient.T, own_wide, precision=lax.Precision.HIGHEST),
        "dp",
        scatter_dimension=0,
        tiled=True,
    )
    embedding_gradient = (row_piece + column_piece) / SOFTMAX_TEMP
    along = lax.psum(jnp.sum(own_wide * embedding_gradient, axis=1), "sp")
    grads = (embedding_gradient - own_wide * along[:, None]) / radius
    return (embeddings, grads)


def solution(mesh):
    return jax.shard_map(
        per_device,
        mesh=mesh,
        in_specs=(
            P(("dp", "sp"), None),
            P(("dp", "sp"), None),
            P(("dp", "sp"), None),
            P("dp", None),
            P("dp"),
        ),
        out_specs=(P("dp", "sp"), P("dp", "sp")),
        check_vma=False,
    )
```

profile of v0, /device:TPU:1, one launch (start us, length us, event | category | flops | bytes accessed | tf_op | source)
XLA Modules:
  0.0 609.4 jit_solution(10150888393768222687)
XLA Ops:
  7.2 1.1 pad_maximum_fusion
  8.3 0.9 copy.28
  9.1 4.8 all-to-all-start.1
  14.0 2.5 copy.26
  16.9 19.7 %reduce = bf16[3584,128]{1,0:T(8,128)(2,1)S(1)} reduce(bf16[3584,1,128]{2,1,0:T(2,128)(2,1)S(1)} %bitcast.49, bf16[]{:T(256)} %broadcast.27), dimensions={1}, to_apply=%bitcast.28.reduce_sub_computation | reduce | bytes 1835010
  36.6 1.6 reshape.59
  38.2 4.2 all-to-all-start
  43.8 7.7 %all-to-all-done = bf16[4,2,57344]{2,1,0:T(2,128)(2,1)S(1)} async-done(((bf16[4,2,57344]{2,1,0:T(2,128)(2,1)}), bf16[4,2,57344]{2,1,0:T(2,128)(2,1)S(1)}, u32[]{:S(2)}, u32[]{:S(2)}) %all-to-all-start) | async-done | bytes 917536 | tf_op jit(solution)/shard_map/all_to_all | solution.py:53
  51.5 0.8 reshape.60
  52.5 0.6 copy.27
  53.1 0.9 reshape_reshape_squeeze.3
  54.3 6.9 %while.10 = (s32[]{:T(128)}, bf16[7,512,128]{2,1,0:T(8,128)(2,1)S(1)}, s32[7,512]{1,0:T(8,128)S(1)}, s32[512]{0:T(512)S(1)}, bf16[7,512,128]{2,1,0:T(8,128)(2,1)...) while((s32[]{:T(128)}, bf16[7,512,128]{2,1,0:T(8,128)(2,1)S(1)}, ...), condition=%wide.region_5.6_spmd, body=%wide.region_2.5_spmd.sunk | while | flops 136641536 | bytes 3688545 | solution.py:40
  61.2 0.9 reshape_reshape.7
  62.4 6.9 %psum.21 = f32[8]{0:T(128)S(1)} all-reduce(f32[8]{0:T(128)S(1)} %get-tuple-element.60), channel_id=1, replica_groups=mesh['dp'=128,'sp'=4] {'sp'}, use_global_device_ids=true, to_apply=%region_7.8 | all-reduce | flops 8 | bytes 64 | tf_op jit(solution)/shard_map/psum | solution.py:62
  69.3 0.7 divide_convert_fusion.2
  70.1 149.2 %all-gather.2.cloned.1.call-done = bf16[1024,896]{1,0:T(8,128)(2,1)} async-done(((bf16[8,896]{1,0:T(8,128)(2,1)}), bf16[1024,896]{1,0:T(8,128)(2,1)}) %all-gather.2.cloned.1.call-update) | async-done | bytes 1835024 | tf_op jit(solution)/shard_map/all_gather | solution.py:65
  219.3 2.1 fusion.21
  221.4 13.3 %psum.22 = f32[8,1024]{1,0:T(8,128)S(1)} all-reduce(f32[8,1024]{1,0:T(8,128)S(1)} %fusion.21), channel_id=1, replica_groups=mesh['dp'=128,'sp'=4] {'sp'}, use_global_device_ids=true, to_apply=%region_8.9 | all-reduce | flops 8192 | bytes 65536 | tf_op jit(solution)/shard_map/psum | solution.py:69
  235.1 3.6 fusion.18
  238.6 1.4 dynamic-slice
  240.7 351.0 %all-reduce.3.cloned.1.call-done = f32[1024,896]{1,0:T(8,128)} async-done(((f32[1024,896]{1,0:T(8,128)}), f32[1024,896]{1,0:T(8,128)}) %all-reduce.3.cloned.1.call-update) | async-done | bytes 3670032
  591.7 1.7 fusion.11
  593.5 8.4 %psum.23 = f32[8]{0:T(128)S(1)} all-reduce(f32[8]{0:T(128)S(1)} %get-tuple-element.62), channel_id=1, replica_groups=mesh['dp'=128,'sp'=4] {'sp'}, use_global_device_ids=true, to_apply=%region_13.14 | all-reduce | flops 8 | bytes 64 | tf_op jit(solution)/shard_map/psum | solution.py:87
  601.9 0.7 fusion.13
  (61 shorter events, 9.8 us)
Async XLA Ops:
  7.2 6.8 %copy-start.2 = (bf16[128,3584]{1,0:T(8,128)(2,1)S(1)}, bf16[128,3584]{1,0:T(8,128)(2,1)}, u32[]{:S(2)}) copy-start(bf16[128,3584]{1,0:T(8,128)(2,1)} %param.7) | copy-start | bytes 2752516
  9.1 29.1 %all-to-all-start.1 = ((bf16[2,128,512]{1,0,2:T(2,128)(2,1)}), bf16[2,128,512]{1,0,2:T(2,128)(2,1)S(1)}, u32[]{:S(2)}, u32[]{:S(2)}) async-start(bf16[2,128,512]{1,0,2:T(2,128)(2,1)} %copy.28), calls=%async_computation.1 | async-start | bytes 524288 | tf_op jit(solution)/shard_map/all_to_all | solution.py:54
  36.6 5.9 copy-start.5
  38.2 13.3 %all-to-all-start = ((bf16[4,2,57344]{2,1,0:T(2,128)(2,1)}), bf16[4,2,57344]{2,1,0:T(2,128)(2,1)S(1)}, u32[]{:S(2)}, u32[]{:S(2)}) async-start(bf16[4,2,57344]{2,1,0:T(2,128)(2,1)} %reshape.59), calls=%async_computation | async-start | bytes 1835008 | tf_op jit(solution)/shard_map/all_to_all | solution.py:53
  42.5 176.9 %all-gather.2.cloned.1.call-start = ((), (), s32[]{:S(2)}) async-start(), calls=%async_computation.2 | async-start | bytes 1849344 | tf_op jit(solution)/shard_map/all_gather | solution.py:65
  53.1 1.2 copy-start.1
  62.1 173.0 %copy-start.4 = (s32[8]{0:T(128)S(1)}, s32[8]{0:T(128)}, u32[]{:S(2)}) copy-start(s32[8]{0:T(128)} %param.11) | copy-start | bytes 100
  70.0 165.0 %copy-start.3 = (bf16[8,896]{1,0:T(8,128)(2,1)S(1)}, bf16[8,896]{1,0:T(8,128)(2,1)}, u32[]{:S(2)}) copy-start(bf16[8,896]{1,0:T(8,128)(2,1)} %divide_convert_fusion.2) | copy-start | bytes 43012
  70.1 521.7 %all-reduce.3.cloned.1.call-start = ((), (), s32[]{:S(2)}) async-start(), calls=%async_computation.3 | async-start | bytes 7340032
  238.6 353.1 %copy-start = (bf16[1024,896]{1,0:T(8,128)(2,1)S(1)}, bf16[1024,896]{1,0:T(8,128)(2,1)}, u32[]{:S(2)}) copy-start(bf16[1024,896]{1,0:T(8,128)(2,1)} %all-gather.2.cloned.1.call-done) | copy-start | bytes 5505028
Sparse Core Ops, SparseCore 0:
  70.2 149.0 all-gather.1
  238.8 352.9 all-reduce.2
where the time goes:
time: 612 us; the launch traced here: 609 us
  waiting for transfers between devices  508 us (83%)
  blocking collectives  28.5 us (5%)
  other arithmetic  24.2 us (4%)
  between operations  14.9 us (2%)
  matrix products  13 us (2%)
  local copies, waits for them, and re-layouts  11.6 us (2%)
  starting transfers between devices  9.12 us (1%)
    unnamed x3, waiting for transfers between devices  351 us
    all_gather x1, waiting for transfers between devices, per_device(): every = lax.all_gather(embeddings, 'dp', axis=0, tiled=True)  149 us
    unnamed x1, other arithmetic  19.7 us
    psum x1, blocking collectives, per_device(): score_logits = lax.psum(partial_scores, 'sp') / SOFTMAX_TEMP  13.3 us
  transfers between devices with their start and end apart: 4, of which 3 were waited for; matrix products, arithmetic and copies ran while one was open for 4% of the time, Pallas kernels for 0%

commit v1 on v0

v1 whole, which is shorter than its diff:
```python
import functools
import math

import jax
import jax.numpy as jnp
from jax import lax
from jax.experimental import pallas as pl
from jax.experimental.pallas import tpu as pltpu
from jax.sharding import PartitionSpec as P

MESH = pl.DeviceIdType.MESH
F32 = jnp.float32
BF16 = jnp.bfloat16
NT = (((1,), (1,)), ((), ()))

GROUPS = 4
PER = 7
HEADS = GROUPS * PER
D = 128
DOCS = 8
TOK = 128
WIN = 512
FEAT = PER * D
NX, NY, NZ, NC = 4, 4, 16, 2
PLANE = NY * NC
ROWS = PLANE * DOCS
COLS = NZ * DOCS
INV_TEMP = 50.0
SCALE2 = D ** (-0.5) * math.log2(math.e)

NEAR = (1, -1, 2, -2)
FAR = (5, -5)
FORWARD = {5: (3, 2, -2, 1, -1), -5: (-2, 2, -1, 1)}


def split2(a):
    hi = a.astype(BF16)
    return hi, (a - hi.astype(F32)).astype(BF16)


def kernel(
    lens, pair, q_hbm, k_hbm, v_hbm, emb_out, grad_out,
    qv, kb, vb, bias, pst, mst, lst, wo, wi, pooled, ucol, urow, prow,
    dsend, drecv, ssend, scol, rsend, srow, gsend, grecv, norms,
    lsem, k_s, k_r, v_s, v_r, w_s, w_r, p_s, p_r, u_s, u_r, c_s, c_r, d_s, d_r, t_s, t_r, a_s, a_r, g_s, g_r,
):
    dp = lax.axis_index("dp")
    x = lax.axis_index("sp")
    c = lax.rem(dp, NC)
    z = lax.rem(dp // NC, NZ)
    y = dp // (NC * NZ)
    mine = y * NC + c

    def at_x(d):
        return (dp, lax.rem(x + d, NX))

    def at_z(o):
        return ((y * NZ + lax.rem(z + o + NZ, NZ)) * NC + c, x)

    def at_plane(k):
        there_y, there_c = lax.rem(y + k // NC, NY), lax.rem(c + k % NC, NC)
        return ((there_y * NZ + z) * NC + there_c, x)

    def slot_to(k):
        return lax.rem(y + k // NC, NY) * NC + lax.rem(c + k % NC, NC)

    def slot_from(k):
        return lax.rem(y - k // NC + NY, NY) * NC + lax.rem(c + k % NC, NC)

    def z_from(o):
        return lax.rem(z - o + NZ, NZ)

    def x_from(d):
        return lax.rem(x - d + NX, NX)

    def copy(src, dst, ss, rs, there):
        return pltpu.make_async_remote_copy(
            src_ref=src, dst_ref=dst, send_sem=ss, recv_sem=rs, device_id=there, device_id_type=MESH
        )

    barrier = pltpu.get_barrier_semaphore()
    for d in range(1, NX):
        pl.semaphore_signal(barrier, inc=1, device_id=at_x(d), device_id_type=MESH)
    for k in range(1, PLANE):
        pl.semaphore_signal(barrier, inc=1, device_id=at_plane(k), device_id_type=MESH)
    for o in range(1, NZ):
        pl.semaphore_signal(barrier, inc=1, device_id=at_z(o), device_id_type=MESH)

    q_in = pltpu.make_async_copy(q_hbm, qv, lsem.at[0])
    k_in = pltpu.make_async_copy(k_hbm, kb.at[x], lsem.at[1])
    v_in = pltpu.make_async_copy(v_hbm.at[:, pl.ds(pl.multiple_of(x * D, D), D)], vb.at[x], lsem.at[2])
    k_in.start()
    q_in.start()
    v_in.start()

    ends = []
    total = 0
    for i in range(DOCS):
        total = total + lens[0, i]
        ends.append(total)

    def segment(places):
        out = jnp.zeros(places.shape, jnp.int32)
        for end in ends:
            out = out + (places >= end).astype(jnp.int32)
        return out

    def iota(shape, axis):
        return lax.broadcasted_iota(jnp.int32, shape, axis)

    q_segment = segment(x * TOK + iota((TOK, TOK), 1))
    row8 = iota((DOCS, D), 0)
    length = jnp.zeros((DOCS, D), F32)
    partner = jnp.zeros((DOCS, D), F32)
    for i in range(DOCS):
        length = jnp.where(row8 == i, lens[0, i].astype(F32), length)
        partner = jnp.where(row8 == i, pair[i].astype(F32), partner)
    prow[mine] = partner
    mst[...] = jnp.zeros_like(mst)
    lst[...] = jnp.ones_like(lst)

    def scores(e):
        block = x_from(e)
        k_segment = segment(block * TOK + iota((TOK, TOK), 0))
        bias[...] = jnp.where(k_segment == q_segment, 0.0, -1e30).astype(F32)

        def group(g, carry):
            key = kb[block, :, pl.ds(pl.multiple_of(g * D, D), D)]
            for j in range(PER):
                query = qv[:, pl.ds(pl.multiple_of((g * PER + j) * D, D), D)]
                s = lax.dot_general(key, query, NT, preferred_element_type=F32) * SCALE2 + bias[...]
                m = jnp.max(s, axis=0, keepdims=True)
                p = jnp.exp2(s - m)
                pst[e, g * PER + j] = p.astype(BF16)
                mst[e, g, j : j + 1, :] = m
                lst[e, g, j : j + 1, :] = jnp.sum(p, axis=0, keepdims=True)
            return carry

        lax.fori_loop(0, GROUPS, group, 0)

    k_in.wait()
    q_in.wait()
    v_in.wait()
    scores(0)

    pl.semaphore_wait(barrier, NX - 1 + PLANE - 1 + NZ - 1)

    k_copies = {d: copy(k_hbm, kb.at[x], k_s.at[d], k_r.at[d], at_x(d)) for d in (1, 3, 2)}
    v_copies = {}
    p_copies = {}
    for d in k_copies:
        k_copies[d].start()
    for d in (1, 3, 2):
        there = lax.rem(x + d, NX)
        v_copies[d] = copy(
            v_hbm.at[:, pl.ds(pl.multiple_of(there * D, D), D)], vb.at[x], v_s.at[d], v_r.at[d], at_x(d)
        )
        v_copies[d].start()
    for k in range(1, PLANE):
        p_copies[k] = copy(prow.at[mine], prow.at[mine], p_s.at[k], p_r.at[k], at_plane(k))
        p_copies[k].start()

    for d in (1, 3, 2):
        k_copies[d].wait_recv()
        scores(d)

    row16 = lax.rem(iota((2 * DOCS, TOK), 0), DOCS)

    def weigh(g, carry):
        ms = [mst[e, g] for e in range(NX)]
        top = functools.reduce(jnp.maximum, ms)
        fs = [jnp.exp2(m - top) for m in ms]
        inv = 1.0 / sum(lst[e, g] * fs[e] for e in range(NX))
        for e in range(NX):
            f = fs[e] * inv
            hi = f.astype(BF16).astype(F32)
            both = jnp.concatenate([hi, f - hi], axis=0)
            acc = jnp.zeros((2 * DOCS, TOK), F32)
            for j in range(PER):
                one = jnp.where(row16 == j, both, 0.0).astype(BF16)
                acc = acc + lax.dot_general(one, pst[e, g * PER + j], NT, preferred_element_type=F32)
            wo[g, :, pl.ds(pl.multiple_of(x_from(e) * TOK, TOK), TOK)] = acc[:DOCS] + acc[DOCS:]
        return carry

    lax.fori_loop(0, GROUPS, weigh, 0)

    w_copies = {
        d: copy(wo.at[lax.rem(x + d, NX)], wi.at[x], w_s.at[d], w_r.at[d], at_x(d)) for d in (2, 1, 3)
    }
    for d in w_copies:
        w_copies[d].start()
    onehot = (segment(iota((DOCS, WIN), 1)) == iota((DOCS, WIN), 0)).astype(F32)
    for d in (1, 3, 2):
        v_copies[d].wait_recv()
    weights = wo[x]
    for d in (1, 3, 2):
        w_copies[d].wait_recv()
        weights = weights + wi[x_from(d)]
    lhs = jnp.concatenate([weights[j : j + 1] * onehot for j in range(PER)], axis=0)
    hi, lo = split2(lhs)
    value = vb[...].reshape(WIN, D)
    sums = jnp.dot(hi, value, preferred_element_type=F32) + jnp.dot(lo, value, preferred_element_type=F32)
    for j in range(PER):
        pooled[:, j * D : (j + 1) * D] = sums[j * DOCS : (j + 1) * DOCS] / length
    short = pooled[...].astype(BF16)
    ucol[z] = short
    urow[mine] = short

    c_copies = {}
    u_copies = {}

    def send_col(origin, step, offset):
        c_copies[offset] = copy(ucol.at[origin], ucol.at[origin], c_s.at[offset % NZ], c_r.at[offset % NZ], at_z(step))
        c_copies[offset].start()

    for o in FAR + NEAR:
        send_col(z, o, o)
    for k in range(1, PLANE):
        u_copies[k] = copy(urow.at[mine], urow.at[mine], u_s.at[k], u_r.at[k], at_plane(k))
        u_copies[k].start()
    for o in FAR:
        c_copies[o].wait_recv()
        for step in FORWARD[o]:
            send_col(z_from(o), step, o + step)
    for k in range(1, PLANE):
        u_copies[k].wait_recv()
    for o in c_copies:
        if o not in FAR:
            c_copies[o].wait_recv()

    rows = urow[...].reshape(ROWS, FEAT)
    cols = ucol[...].reshape(COLS, FEAT)

    def squares(a):
        wide = a.astype(F32)
        hi, lo = split2(wide * wide)
        ones = jnp.ones((2 * DOCS, FEAT), BF16)
        return (
            lax.dot_general(ones, hi, NT, preferred_element_type=F32)
            + lax.dot_general(ones, lo, NT, preferred_element_type=F32)
        )[:DOCS]

    dsend[:ROWS, :] = lax.dot_general(rows, cols, NT, preferred_element_type=F32)
    dsend[ROWS:, :] = jnp.where(row8 == 0, squares(cols), squares(jnp.concatenate([rows, rows], axis=0)))
    d_copies = {d: copy(dsend, drecv.at[x], d_s.at[d], d_r.at[d], at_x(d)) for d in (2, 1, 3)}
    for d in d_copies:
        d_copies[d].start()
    for d in (1, 3, 2):
        d_copies[d].wait_recv()
    full = dsend[...]
    for d in range(1, NX):
        full = full + drecv[x_from(d)]

    r_id, c_id = iota((ROWS, COLS), 0), iota((ROWS, COLS), 1)
    eye = r_id == c_id

    def to_column(row):
        return jnp.sum(jnp.where(eye, row, 0.0), axis=1, keepdims=True)

    radius = jnp.sqrt(to_column(full[ROWS + 1 : ROWS + 2]) + 1e-6)
    norms[...] = jnp.broadcast_to(radius, (ROWS, D))
    inv_cols = 1.0 / jnp.sqrt(full[ROWS : ROWS + 1] + 1e-6)
    logits = full[:ROWS] * ((1.0 / radius) * (inv_cols * INV_TEMP))
    r_plane, r_doc = r_id // DOCS, lax.rem(r_id, DOCS)
    c_z, c_doc = c_id // DOCS, lax.rem(c_id, DOCS)
    same = (r_plane == mine) & (c_z == z) & (r_doc == c_doc)
    weight = jnp.where(same, 0.0, jnp.exp(logits))
    col_sum = jnp.sum(weight, axis=0, keepdims=True)
    row_sum = jnp.sum(jnp.where(eye, jnp.sum(weight, axis=1, keepdims=True), 0.0), axis=0, keepdims=True)
    ssend[...] = jnp.broadcast_to(col_sum, (DOCS, D))
    rsend[...] = jnp.broadcast_to(row_sum, (DOCS, D))
    t_copies = {}
    a_copies = {}
    for o in (8, 7, -7, 6, -6, 5, -5, 4, -4, 3, -3, 2, -2, 1, -1):
        t_copies[o] = copy(ssend.at[pl.ds(0, 1)], scol.at[z, pl.ds(0, 1)], t_s.at[o % NZ], t_r.at[o % NZ], at_z(o))
        t_copies[o].start()
    for k in range(1, PLANE):
        a_copies[k] = copy(rsend.at[pl.ds(0, 1)], srow.at[mine, pl.ds(0, 1)], a_s.at[k], a_r.at[k], at_plane(k))
        a_copies[k].start()

    own_radius = norms[pl.ds(pl.multiple_of(mine * DOCS, DOCS), DOCS), :]
    for j in range(PER):
        at = slice(j * D, (j + 1) * D)
        emb_out[:, at] = (pooled[:, at] / own_radius).astype(BF16)
    partners = prow_wait(p_copies, prow).reshape(ROWS, D)
    column_doc = ((y * NZ + c_z) * NC + c) * DOCS + c_doc
    pairs = jnp.where(partners == column_doc.astype(F32), 2.0, 0.0)
    for k in range(1, PLANE):
        a_copies[k].wait_recv()
        row_sum = row_sum + srow[slot_from(k), 0:1, :]
    for o in t_copies:
        t_copies[o].wait_recv()
        col_sum = col_sum + scol[z_from(o), 0:1, :]
    coef = weight * (1.0 / to_column(row_sum) + 1.0 / col_sum) - pairs
    along = jnp.sum(coef * logits, axis=1, keepdims=True)
    scaled = coef * (inv_cols * INV_TEMP)
    hi = scaled.astype(BF16)
    rest = scaled - hi.astype(F32)
    mid, lo = split2(rest)
    piece = (
        jnp.dot(hi, cols, preferred_element_type=F32)
        + jnp.dot(mid, cols, preferred_element_type=F32)
        + jnp.dot(lo, cols, preferred_element_type=F32)
    )
    gsend[:, :, :FEAT] = piece.reshape(PLANE, DOCS, FEAT)
    gsend[:, :, FEAT:] = jnp.broadcast_to(along, (ROWS, D)).reshape(PLANE, DOCS, D)
    g_copies = {}
    for k in range(PLANE - 1, 0, -1):
        g_copies[k] = copy(gsend.at[slot_to(k)], grecv.at[mine], g_s.at[k], g_r.at[k], at_plane(k))
        g_copies[k].start()
    gradient = gsend[mine]
    for k in range(1, PLANE):
        g_copies[k].wait_recv()
        gradient = gradient + grecv[slot_from(k)]
    projection = gradient[:, FEAT:]
    for j in range(PER):
        at = slice(j * D, (j + 1) * D)
        own = emb_out[:, at].astype(F32)
        grad_out[:, at] = (gradient[:, at] - own * projection) / own_radius

    for copies in (k_copies, v_copies, p_copies, w_copies, c_copies, u_copies, d_copies, t_copies, a_copies, g_copies):
        for key in copies:
            copies[key].wait_send()


def prow_wait(p_copies, prow):
    for k in p_copies:
        p_copies[k].wait_recv()
    return prow[...]


def per_device(queries, keys, values, document_lengths, pair_ids):
    dma = pltpu.SemaphoreType.DMA
    vmem = pl.BlockSpec(memory_space=pltpu.VMEM)
    smem = pl.BlockSpec(memory_space=pltpu.SMEM)
    hbm = pl.BlockSpec(memory_space=pl.ANY)
    return pl.pallas_call(
        kernel,
        out_shape=(jax.ShapeDtypeStruct((DOCS, FEAT), BF16), jax.ShapeDtypeStruct((DOCS, FEAT), F32)),
        in_specs=[smem, smem, hbm, hbm, hbm],
        out_specs=(vmem, vmem),
        scratch_shapes=[
            pltpu.VMEM((TOK, HEADS * D), BF16),
            pltpu.VMEM((NX, TOK, GROUPS * D), BF16),
            pltpu.VMEM((NX, TOK, D), BF16),
            pltpu.VMEM((TOK, TOK), F32),
            pltpu.VMEM((NX, HEADS, TOK, TOK), BF16),
            pltpu.VMEM((NX, GROUPS, DOCS, TOK), F32),
            pltpu.VMEM((NX, GROUPS, DOCS, TOK), F32),
            pltpu.VMEM((GROUPS, DOCS, WIN), F32),
            pltpu.VMEM((NX, DOCS, WIN), F32),
            pltpu.VMEM((DOCS, FEAT), F32),
            pltpu.VMEM((NZ, DOCS, FEAT), BF16),
            pltpu.VMEM((PLANE, DOCS, FEAT), BF16),
            pltpu.VMEM((PLANE, DOCS, D), F32),
            pltpu.VMEM((ROWS + DOCS, COLS), F32),
            pltpu.VMEM((NX, ROWS + DOCS, COLS), F32),
            pltpu.VMEM((DOCS, D), F32),
            pltpu.VMEM((NZ, DOCS, D), F32),
            pltpu.VMEM((DOCS, D), F32),
            pltpu.VMEM((PLANE, DOCS, D), F32),
            pltpu.VMEM((PLANE, DOCS, FEAT + D), F32),
            pltpu.VMEM((PLANE, DOCS, FEAT + D), F32),
            pltpu.VMEM((ROWS, D), F32),
            dma((3,)),
            dma((NX,)), dma((NX,)),
            dma((NX,)), dma((NX,)),
            dma((NX,)), dma((NX,)),
            dma((PLANE,)), dma((PLANE,)),
            dma((PLANE,)), dma((PLANE,)),
            dma((NZ,)), dma((NZ,)),
            dma((NX,)), dma((NX,)),
            dma((NZ,)), dma((NZ,)),
            dma((PLANE,)), dma((PLANE,)),
            dma((PLANE,)), dma((PLANE,)),
        ],
        compiler_params=pltpu.CompilerParams(
            collective_id=0, has_side_effects=True, vmem_limit_bytes=32 << 20
        ),
    )(document_lengths, pair_ids, queries, keys, values)


def solution(mesh):
    return jax.shard_map(
        per_device,
        mesh=mesh,
        in_specs=(
            P(("dp", "sp"), None),
            P(("dp", "sp"), None),
            P(("dp", "sp"), None),
            P("dp", None),
            P("dp"),
        ),
        out_specs=(P("dp", "sp"), P("dp", "sp")),
        check_vma=False,
    )
```

time: 612 us -> 69.7 us (0.11)
  waiting for transfers between devices: 508 us -> 0 us
  Pallas kernels: 0 us -> 63.3 us
  blocking collectives: 28.5 us -> 0 us
  other arithmetic: 24.2 us -> 0 us
  between operations: 14.9 us -> 0.65 us
  matrix products: 13 us -> 0 us
  starting transfers between devices: 9.12 us -> 0 us
    unnamed x3 -> x0, waiting for transfers between devices: 351 us -> none
    all_gather x1 -> x0, waiting for transfers between devices: 149 us -> none  [per_device(): every = lax.all_gather(embeddings, 'dp', axis=0, tiled=True)]
    pallas_call x0 -> x1, Pallas kernels: none -> 63.3 us  [per_device(): pl.pallas_call(kernel, out_shape=(jax.ShapeDtypeStruct((DOCS, FEAT), BF16...]
    psum x3 -> x0, blocking collectives: 28.5 us -> none  [the longest x1 13.3 us: per_device(): score_logits = lax.psum(partial_scores, 'sp') / SOFTMAX_TEMP]
    unnamed x1 -> x0, other arithmetic: 19.7 us -> none
    dot_general x18 -> x0, matrix products: 13 us -> none  [the longest x1 3.55 us: per_device(): jnp.dot(loss_coefficient.T, own_wide, precision=lax.Precision.HIGHEST)]
    all_to_all x2 -> x0, starting transfers between devices: 9.08 us -> none  [the longest x1 4.84 us: per_device(): lax.all_to_all(stacked, 'sp', split_axis=2, concat_axis=1, tiled=True)]
    all_to_all x2 -> x0, waiting for transfers between devices: 7.71 us -> none  [the longest x1 7.71 us: per_device(): lax.all_to_all(queries[None], 'sp', split_axis=2, concat_axis=1, tiled=True)]
  transfers between devices with their start and end apart: 4 -> 0, of which waited for: 3 -> 0; matrix products, arithmetic and copies ran while one was open for 4% -> 0% of each run, Pallas kernels for 0% -> 0%
where the time goes in v1:
time: 69.7 us; the launch traced here: 69.5 us
  Pallas kernels  63.3 us (91%)
  local copies, waits for them, and re-layouts  5.5 us (8%)
    pallas_call x1, Pallas kernels, per_device(): pl.pallas_call(kernel, out_shape=(jax.ShapeDtypeStruct((DOCS, FEAT), BF16...  63.3 us
    unnamed x12, local copies, waits for them, and re-layouts  5.5 us

profile of v1, /device:TPU:1, one launch (start us, length us, event | category | flops | bytes accessed | tf_op | source)
XLA Modules:
  0.0 69.5 jit_solution(3643481125148598917)
XLA Ops:
  0.6 0.0 copy-start
  0.6 1.2 %copy-done = bf16[128,3584]{1,0:T(8,128)(2,1)S(1)} copy-done((bf16[128,3584]{1,0:T(8,128)(2,1)S(1)}, bf16[128,3584]{1,0:T(8,128)(2,1)}, u32[]{:S(2)}) %copy-start) | copy-done | bytes 917528
  1.8 0.0 copy-start.1
  1.8 0.9 %copy-done.1 = bf16[128,512]{1,0:T(8,128)(2,1)S(1)} copy-done((bf16[128,512]{1,0:T(8,128)(2,1)S(1)}, bf16[128,512]{1,0:T(8,128)(2,1)}, u32[]{:S(2)}) %copy-start.1) | copy-done | bytes 131096
  2.7 0.0 copy-start.2
  2.7 0.9 %copy-done.2 = bf16[128,512]{1,0:T(8,128)(2,1)S(1)} copy-done((bf16[128,512]{1,0:T(8,128)(2,1)S(1)}, bf16[128,512]{1,0:T(8,128)(2,1)}, u32[]{:S(2)}) %copy-start.2) | copy-done | bytes 131096
  3.6 0.0 copy-start.3
  3.6 0.7 copy-done.3
  4.3 0.0 copy-start.4
  4.3 0.7 copy-done.4
  4.9 63.3 %shard_map.68 = (bf16[8,896]{1,0:T(8,128)(2,1)S(1)}, f32[8,896]{1,0:T(8,128)S(1)}) custom-call(s32[1,8]{1,0:T(1,128)S(1)} %copy-done.3, s32[8]{0:T(128)S(1)} %copy-done.4, bf16[128,3584]{1,0:T(8,128)(2,1)S(1)} %copy-done, bf16[128,512]{1,0:T(8,128)(2,1)S(1)} %copy-done.1, bf16[128,512]{1,0:T(8,128)(2,1)S(1)} %copy-done.2), custom_call_target="tpu_custom_call" | custom-call | tf_op jit(solution)/shard_map/pallas_call | solution.py:337
  68.2 0.6 copy.9
  68.8 0.6 copy.10
Async XLA Ops:
  0.6 1.2 %copy-start = (bf16[128,3584]{1,0:T(8,128)(2,1)S(1)}, bf16[128,3584]{1,0:T(8,128)(2,1)}, u32[]{:S(2)}) copy-start(bf16[128,3584]{1,0:T(8,128)(2,1)} %q_hbm.1) | copy-start | bytes 2752516
  1.8 0.9 %copy-start.1 = (bf16[128,512]{1,0:T(8,128)(2,1)S(1)}, bf16[128,512]{1,0:T(8,128)(2,1)}, u32[]{:S(2)}) copy-start(bf16[128,512]{1,0:T(8,128)(2,1)} %k_hbm.1) | copy-start | bytes 393220
  2.7 0.9 %copy-start.2 = (bf16[128,512]{1,0:T(8,128)(2,1)S(1)}, bf16[128,512]{1,0:T(8,128)(2,1)}, u32[]{:S(2)}) copy-start(bf16[128,512]{1,0:T(8,128)(2,1)} %v_hbm.1) | copy-start | bytes 393220
  3.6 0.7 copy-start.3
  4.3 0.7 copy-start.4

commit v2 on v1

--- a/solution.py
+++ b/solution.py
@@ -39,8 +39,8 @@
 
 
 def kernel(
-    lens, pair, q_hbm, k_hbm, v_hbm, emb_out, grad_out,
-    qv, kb, vb, bias, pst, mst, lst, wo, wi, pooled, ucol, urow, prow,
+    lens_hbm, pair_hbm, q_hbm, k_hbm, v_hbm, out,
+    lens, pair, qv, kb, vb, bias, pst, mst, lst, wo, wi, pooled, ucol, urow, prow,
     dsend, drecv, ssend, scol, rsend, srow, gsend, grecv, norms,
     lsem, k_s, k_r, v_s, v_r, w_s, w_r, p_s, p_r, u_s, u_r, c_s, c_r, d_s, d_r, t_s, t_r, a_s, a_r, g_s, g_r,
 ):
@@ -86,12 +86,21 @@
     for o in range(1, NZ):
         pl.semaphore_signal(barrier, inc=1, device_id=at_z(o), device_id_type=MESH)
 
-    q_in = pltpu.make_async_copy(q_hbm, qv, lsem.at[0])
-    k_in = pltpu.make_async_copy(k_hbm, kb.at[x], lsem.at[1])
-    v_in = pltpu.make_async_copy(v_hbm.at[:, pl.ds(pl.multiple_of(x * D, D), D)], vb.at[x], lsem.at[2])
-    k_in.start()
+    lens_in = pltpu.make_async_copy(lens_hbm, lens, lsem.at[0])
+    pair_in = pltpu.make_async_copy(pair_hbm, pair, lsem.at[1])
+    q_in = pltpu.make_async_copy(q_hbm, qv, lsem.at[2])
+    v_in = pltpu.make_async_copy(v_hbm.at[:, pl.ds(pl.multiple_of(x * D, D), D)], vb.at[x], lsem.at[3])
+    k_in = [
+        pltpu.make_async_copy(k_hbm.at[:, g * D : (g + 1) * D], kb.at[g, x], lsem.at[4 + g]) for g in range(GROUPS)
+    ]
+    lens_in.start()
+    pair_in.start()
+    for one in k_in:
+        one.start()
     q_in.start()
     v_in.start()
+    lens_in.wait()
+    pair_in.wait()
 
     ends = []
     total = 0
@@ -119,37 +128,34 @@
     mst[...] = jnp.zeros_like(mst)
     lst[...] = jnp.ones_like(lst)
 
-    def scores(e):
-        block = x_from(e)
-        k_segment = segment(block * TOK + iota((TOK, TOK), 0))
-        bias[...] = jnp.where(k_segment == q_segment, 0.0, -1e30).astype(F32)
-
-        def group(g, carry):
-            key = kb[block, :, pl.ds(pl.multiple_of(g * D, D), D)]
-            for j in range(PER):
-                query = qv[:, pl.ds(pl.multiple_of((g * PER + j) * D, D), D)]
-                s = lax.dot_general(key, query, NT, preferred_element_type=F32) * SCALE2 + bias[...]
-                m = jnp.max(s, axis=0, keepdims=True)
-                p = jnp.exp2(s - m)
-                pst[e, g * PER + j] = p.astype(BF16)
-                mst[e, g, j : j + 1, :] = m
-                lst[e, g, j : j + 1, :] = jnp.sum(p, axis=0, keepdims=True)
-            return carry
-
-        lax.fori_loop(0, GROUPS, group, 0)
-
-    k_in.wait()
-    q_in.wait()
-    v_in.wait()
-    scores(0)
-
+    for e in range(NX):
+        k_segment = segment(x_from(e) * TOK + iota((TOK, TOK), 0))
+        bias[e] = jnp.where(k_segment == q_segment, 0.0, -1e30).astype(F32)
+
+    def scores(e, g):
+        key = kb[g, x_from(e)]
+        for j in range(PER):
+            query = qv[:, pl.ds(pl.multiple_of((g * PER + j) * D, D), D)]
+            s = lax.dot_general(key, query, NT, preferred_element_type=F32) * SCALE2 + bias[e]
+            m = jnp.max(s, axis=0, keepdims=True)
+            p = jnp.exp2(s - m)
+            pst[e, g, :, j * TOK : (j + 1) * TOK] = p.astype(BF16)
+            mst[e, g, j : j + 1, :] = m
+            lst[e, g, j : j + 1, :] = jnp.sum(p, axis=0, keepdims=True)
+
+    for one in k_in:
+        one.wait()
     pl.semaphore_wait(barrier, NX - 1 + PLANE - 1 + NZ - 1)
 
-    k_copies = {d: copy(k_hbm, kb.at[x], k_s.at[d], k_r.at[d], at_x(d)) for d in (1, 3, 2)}
+    k_copies = {}
     v_copies = {}
     p_copies = {}
-    for d in k_copies:
-        k_copies[d].start()
+    w_copies = {}
+    for i in range(GROUPS):
+        for d in (1, 3, 2):
+            g = lax.rem(x + d + 1 + i, GROUPS)
+            k_copies[d, i] = copy(kb.at[g, x], kb.at[g, x], k_s.at[d, i], k_r.at[d, i], at_x(d))
+            k_copies[d, i].start()
     for d in (1, 3, 2):
         there = lax.rem(x + d, NX)
         v_copies[d] = copy(
@@ -159,14 +165,18 @@
     for k in range(1, PLANE):
         p_copies[k] = copy(prow.at[mine], prow.at[mine], p_s.at[k], p_r.at[k], at_plane(k))
         p_copies[k].start()
-
-    for d in (1, 3, 2):
-        k_copies[d].wait_recv()
-        scores(d)
+    q_in.wait()
+    v_in.wait()
+
+    def own(g, carry):
+        scores(0, g)
+        return carry
+
+    lax.fori_loop(0, GROUPS, own, 0)
 
     row16 = lax.rem(iota((2 * DOCS, TOK), 0), DOCS)
 
-    def weigh(g, carry):
+    def weigh(g):
         ms = [mst[e, g] for e in range(NX)]
         top = functools.reduce(jnp.maximum, ms)
         fs = [jnp.exp2(m - top) for m in ms]
@@ -175,20 +185,19 @@
             f = fs[e] * inv
             hi = f.astype(BF16).astype(F32)
             both = jnp.concatenate([hi, f - hi], axis=0)
-            acc = jnp.zeros((2 * DOCS, TOK), F32)
-            for j in range(PER):
-                one = jnp.where(row16 == j, both, 0.0).astype(BF16)
-                acc = acc + lax.dot_general(one, pst[e, g * PER + j], NT, preferred_element_type=F32)
+            lhs = jnp.concatenate([jnp.where(row16 == j, both, 0.0).astype(BF16) for j in range(PER)], axis=1)
+            acc = lax.dot_general(lhs, pst[e, g], NT, preferred_element_type=F32)
             wo[g, :, pl.ds(pl.multiple_of(x_from(e) * TOK, TOK), TOK)] = acc[:DOCS] + acc[DOCS:]
-        return carry
-
-    lax.fori_loop(0, GROUPS, weigh, 0)
-
-    w_copies = {
-        d: copy(wo.at[lax.rem(x + d, NX)], wi.at[x], w_s.at[d], w_r.at[d], at_x(d)) for d in (2, 1, 3)
-    }
-    for d in w_copies:
-        w_copies[d].start()
+
+    for i in range(GROUPS):
+        group = lax.rem(x + 1 + i, GROUPS)
+        for d in (1, 3, 2):
+            k_copies[d, i].wait_recv()
+            scores(d, group)
+        weigh(group)
+        if i < GROUPS - 1:
+            w_copies[i + 1] = copy(wo.at[group], wi.at[x], w_s.at[i + 1], w_r.at[i + 1], at_x(i + 1))
+            w_copies[i + 1].start()
     onehot = (segment(iota((DOCS, WIN), 1)) == iota((DOCS, WIN), 0)).astype(F32)
     for d in (1, 3, 2):
         v_copies[d].wait_recv()
@@ -281,7 +290,7 @@
     own_radius = norms[pl.ds(pl.multiple_of(mine * DOCS, DOCS), DOCS), :]
     for j in range(PER):
         at = slice(j * D, (j + 1) * D)
-        emb_out[:, at] = (pooled[:, at] / own_radius).astype(BF16)
+        out[:, at] = (pooled[:, at] / own_radius).astype(BF16).astype(F32)
     partners = prow_wait(p_copies, prow).reshape(ROWS, D)
     column_doc = ((y * NZ + c_z) * NC + c) * DOCS + c_doc
     pairs = jnp.where(partners == column_doc.astype(F32), 2.0, 0.0)
@@ -302,23 +311,28 @@
         + jnp.dot(mid, cols, preferred_element_type=F32)
         + jnp.dot(lo, cols, preferred_element_type=F32)
     )
-    gsend[:, :, :FEAT] = piece.reshape(PLANE, DOCS, FEAT)
-    gsend[:, :, FEAT:] = jnp.broadcast_to(along, (ROWS, D)).reshape(PLANE, DOCS, D)
+    high, low = split2(along)
+    first = iota((ROWS, D), 1) < D // 2
+    sides = jnp.where(first, high.astype(F32), low.astype(F32)).astype(BF16)
+    gsend[:, :, :FEAT] = piece.astype(BF16).reshape(PLANE, DOCS, FEAT)
+    gsend[:, :, FEAT:] = sides.reshape(PLANE, DOCS, D)
     g_copies = {}
     for k in range(PLANE - 1, 0, -1):
         g_copies[k] = copy(gsend.at[slot_to(k)], grecv.at[mine], g_s.at[k], g_r.at[k], at_plane(k))
         g_copies[k].start()
-    gradient = gsend[mine]
+    gradient = gsend[mine].astype(F32)
     for k in range(1, PLANE):
         g_copies[k].wait_recv()
-        gradient = gradient + grecv[slot_from(k)]
-    projection = gradient[:, FEAT:]
+        gradient = gradient + grecv[slot_from(k)].astype(F32)
+    tail = gradient[:, FEAT:]
+    projection = tail[:, :1] + tail[:, D // 2 : D // 2 + 1]
     for j in range(PER):
         at = slice(j * D, (j + 1) * D)
-        own = emb_out[:, at].astype(F32)
-        grad_out[:, at] = (gradient[:, at] - own * projection) / own_radius
-
-    for copies in (k_copies, v_copies, p_copies, w_copies, c_copies, u_copies, d_copies, t_copies, a_copies, g_copies):
+        out[:, FEAT + j * D : FEAT + (j + 1) * D] = (gradient[:, at] - out[:, at] * projection) / own_radius
+
+    for copies in (
+        k_copies, v_copies, p_copies, w_copies, c_copies, u_copies, d_copies, t_copies, a_copies, g_copies
+    ):
         for key in copies:
             copies[key].wait_send()
 
@@ -332,19 +346,20 @@
 def per_device(queries, keys, values, document_lengths, pair_ids):
     dma = pltpu.SemaphoreType.DMA
     vmem = pl.BlockSpec(memory_space=pltpu.VMEM)
-    smem = pl.BlockSpec(memory_space=pltpu.SMEM)
     hbm = pl.BlockSpec(memory_space=pl.ANY)
-    return pl.pallas_call(
+    both = pl.pallas_call(
         kernel,
-        out_shape=(jax.ShapeDtypeStruct((DOCS, FEAT), BF16), jax.ShapeDtypeStruct((DOCS, FEAT), F32)),
-        in_specs=[smem, smem, hbm, hbm, hbm],
-        out_specs=(vmem, vmem),
+        out_shape=jax.ShapeDtypeStruct((DOCS, 2 * FEAT), F32),
+        in_specs=[hbm] * 5,
+        out_specs=vmem,
         scratch_shapes=[
+            pltpu.SMEM((1, DOCS), jnp.int32),
+            pltpu.SMEM((DOCS,), jnp.int32),
             pltpu.VMEM((TOK, HEADS * D), BF16),
-            pltpu.VMEM((NX, TOK, GROUPS * D), BF16),
+            pltpu.VMEM((GROUPS, NX, TOK, D), BF16),
             pltpu.VMEM((NX, TOK, D), BF16),
-            pltpu.VMEM((TOK, TOK), F32),
-            pltpu.VMEM((NX, HEADS, TOK, TOK), BF16),
+            pltpu.VMEM((NX, TOK, TOK), F32),
+            pltpu.VMEM((NX, GROUPS, TOK, PER * TOK), BF16),
             pltpu.VMEM((NX, GROUPS, DOCS, TOK), F32),
             pltpu.VMEM((NX, GROUPS, DOCS, TOK), F32),
             pltpu.VMEM((GROUPS, DOCS, WIN), F32),
@@ -359,11 +374,11 @@
             pltpu.VMEM((NZ, DOCS, D), F32),
             pltpu.VMEM((DOCS, D), F32),
             pltpu.VMEM((PLANE, DOCS, D), F32),
-            pltpu.VMEM((PLANE, DOCS, FEAT + D), F32),
-            pltpu.VMEM((PLANE, DOCS, FEAT + D), F32),
+            pltpu.VMEM((PLANE, DOCS, FEAT + D), BF16),
+            pltpu.VMEM((PLANE, DOCS, FEAT + D), BF16),
             pltpu.VMEM((ROWS, D), F32),
-            dma((3,)),
-            dma((NX,)), dma((NX,)),
+            dma((4 + GROUPS,)),
+            dma((NX, GROUPS)), dma((NX, GROUPS)),
             dma((NX,)), dma((NX,)),
             dma((NX,)), dma((NX,)),
             dma((PLANE,)), dma((PLANE,)),
@@ -375,9 +390,10 @@
             dma((PLANE,)), dma((PLANE,)),
         ],
         compiler_params=pltpu.CompilerParams(
-            collective_id=0, has_side_effects=True, vmem_limit_bytes=32 << 20
+            collective_id=0, has_side_effects=True, vmem_limit_bytes=60 << 20
         ),
     )(document_lengths, pair_ids, queries, keys, values)
+    return both[:, :FEAT].astype(BF16), both[:, FEAT:]
 
 
 def solution(mesh):

time: 69.7 us -> 61.8 us (0.89)
  Pallas kernels: 63.3 us -> 58.2 us
  local copies, waits for them, and re-layouts: 5.5 us -> 2.71 us
    unnamed x12 -> x0, local copies, waits for them, and re-layouts: 5.5 us -> none
    pallas_call x1, Pallas kernels: 63.3 us -> 58.2 us  [per_device(): pl.pallas_call(kernel, out_shape=jax.ShapeDtypeStruct((DOCS, 2 * FEAT), F...]
    slice x0 -> x2, local copies, waits for them, and re-layouts: none -> 2.71 us  [per_device(): return (both[:, :FEAT].astype(BF16), both[:, FEAT:])]
where the time goes in v2:
time: 61.8 us; the launch traced here: 61.6 us
  Pallas kernels  58.2 us (94%)
  local copies, waits for them, and re-layouts  2.71 us (4%)
  between operations  0.64 us (1%)
    pallas_call x1, Pallas kernels, per_device(): pl.pallas_call(kernel, out_shape=jax.ShapeDtypeStruct((DOCS, 2 * FEAT), F...  58.2 us
    slice x2, local copies, waits for them, and re-layouts, per_device(): return (both[:, :FEAT].astype(BF16), both[:, FEAT:])  2.71 us

profile of v2, /device:TPU:1, one launch (start us, length us, event | category | flops | bytes accessed | tf_op | source)
XLA Modules:
  0.0 61.6 jit_solution(8081035524605804630)
XLA Ops:
  0.6 58.2 %shard_map.68 = f32[8,1792]{1,0:T(8,128)} custom-call(s32[1,8]{1,0:T(1,128)} %lens_hbm.1, s32[8]{0:T(128)} %pair_hbm.1, bf16[128,3584]{1,0:T(8,128)(2,1)} %q_hbm.1, bf16[128,512]{1,0:T(8,128)(2,1)} %k_hbm.1, bf16[128,512]{1,0:T(8,128)(2,1)} %v_hbm.1), custom_call_target="tpu_custom_call" | custom-call | tf_op jit(solution)/shard_map/pallas_call | solution.py:350
  58.9 1.4 %slice.11 = bf16[8,896]{1,0:T(8,128)(2,1)} slice(f32[8,1792]{1,0:T(8,128)} %shard_map.68), slice={[0:8], [0:896]} | slice | bytes 28672 | tf_op jit(solution)/shard_map/slice | solution.py:396
  60.2 1.4 %slice.8 = f32[8,896]{1,0:T(8,128)} slice(f32[8,1792]{1,0:T(8,128)} %shard_map.68), slice={[0:8], [896:1792]} | slice | bytes 57344 | tf_op jit(solution)/shard_map/slice | solution.py:396

commit v3 on v2

--- a/solution.py
+++ b/solution.py
@@ -30,7 +30,7 @@
 
 NEAR = (1, -1, 2, -2)
 FAR = (5, -5)
-FORWARD = {5: (3, 2, -2, 1, -1), -5: (-2, 2, -1, 1)}
+FORWARD = {5: (2, -2, 1, -1), -5: (-2, 2, -1, 1)}
 
 
 def split2(a):
@@ -42,7 +42,7 @@
     lens_hbm, pair_hbm, q_hbm, k_hbm, v_hbm, out,
     lens, pair, qv, kb, vb, bias, pst, mst, lst, wo, wi, pooled, ucol, urow, prow,
     dsend, drecv, ssend, scol, rsend, srow, gsend, grecv, norms,
-    lsem, k_s, k_r, v_s, v_r, w_s, w_r, p_s, p_r, u_s, u_r, c_s, c_r, d_s, d_r, t_s, t_r, a_s, a_r, g_s, g_r,
+    heard, lsem, k_s, k_r, v_s, v_r, w_s, w_r, p_s, p_r, u_s, u_r, c_s, c_r, d_s, d_r, t_s, t_r, a_s, a_r, g_s, g_r,
 ):
     dp = lax.axis_index("dp")
     x = lax.axis_index("sp")
@@ -83,7 +83,7 @@
         pl.semaphore_signal(barrier, inc=1, device_id=at_x(d), device_id_type=MESH)
     for k in range(1, PLANE):
         pl.semaphore_signal(barrier, inc=1, device_id=at_plane(k), device_id_type=MESH)
-    for o in range(1, NZ):
+    for o in NEAR:
         pl.semaphore_signal(barrier, inc=1, device_id=at_z(o), device_id_type=MESH)
 
     lens_in = pltpu.make_async_copy(lens_hbm, lens, lsem.at[0])
@@ -93,59 +93,15 @@
     k_in = [
         pltpu.make_async_copy(k_hbm.at[:, g * D : (g + 1) * D], kb.at[g, x], lsem.at[4 + g]) for g in range(GROUPS)
     ]
+    for one in k_in:
+        one.start()
     lens_in.start()
     pair_in.start()
-    for one in k_in:
-        one.start()
     q_in.start()
     v_in.start()
-    lens_in.wait()
-    pair_in.wait()
-
-    ends = []
-    total = 0
-    for i in range(DOCS):
-        total = total + lens[0, i]
-        ends.append(total)
-
-    def segment(places):
-        out = jnp.zeros(places.shape, jnp.int32)
-        for end in ends:
-            out = out + (places >= end).astype(jnp.int32)
-        return out
-
-    def iota(shape, axis):
-        return lax.broadcasted_iota(jnp.int32, shape, axis)
-
-    q_segment = segment(x * TOK + iota((TOK, TOK), 1))
-    row8 = iota((DOCS, D), 0)
-    length = jnp.zeros((DOCS, D), F32)
-    partner = jnp.zeros((DOCS, D), F32)
-    for i in range(DOCS):
-        length = jnp.where(row8 == i, lens[0, i].astype(F32), length)
-        partner = jnp.where(row8 == i, pair[i].astype(F32), partner)
-    prow[mine] = partner
-    mst[...] = jnp.zeros_like(mst)
-    lst[...] = jnp.ones_like(lst)
-
-    for e in range(NX):
-        k_segment = segment(x_from(e) * TOK + iota((TOK, TOK), 0))
-        bias[e] = jnp.where(k_segment == q_segment, 0.0, -1e30).astype(F32)
-
-    def scores(e, g):
-        key = kb[g, x_from(e)]
-        for j in range(PER):
-            query = qv[:, pl.ds(pl.multiple_of((g * PER + j) * D, D), D)]
-            s = lax.dot_general(key, query, NT, preferred_element_type=F32) * SCALE2 + bias[e]
-            m = jnp.max(s, axis=0, keepdims=True)
-            p = jnp.exp2(s - m)
-            pst[e, g, :, j * TOK : (j + 1) * TOK] = p.astype(BF16)
-            mst[e, g, j : j + 1, :] = m
-            lst[e, g, j : j + 1, :] = jnp.sum(p, axis=0, keepdims=True)
-
     for one in k_in:
         one.wait()
-    pl.semaphore_wait(barrier, NX - 1 + PLANE - 1 + NZ - 1)
+    pl.semaphore_wait(barrier, NX - 1 + PLANE - 1 + len(NEAR))
 
     k_copies = {}
     v_copies = {}
@@ -162,6 +118,52 @@
             v_hbm.at[:, pl.ds(pl.multiple_of(there * D, D), D)], vb.at[x], v_s.at[d], v_r.at[d], at_x(d)
         )
         v_copies[d].start()
+    for o in (2, -2):
+        pl.semaphore_signal(heard.at[0], inc=1, device_id=at_z(o), device_id_type=MESH)
+    lens_in.wait()
+    pair_in.wait()
+
+    ends = []
+    total = 0
+    for i in range(DOCS):
+        total = total + lens[0, i]
+        ends.append(total)
+
+    def segment(places):
+        out = jnp.zeros(places.shape, jnp.int32)
+        for end in ends:
+            out = out + (places >= end).astype(jnp.int32)
+        return out
+
+    def iota(shape, axis):
+        return lax.broadcasted_iota(jnp.int32, shape, axis)
+
+    q_segment = segment(x * TOK + iota((TOK, TOK), 1))
+    row8 = iota((DOCS, D), 0)
+    length = jnp.zeros((DOCS, D), F32)
+    partner = jnp.zeros((DOCS, D), F32)
+    for i in range(DOCS):
+        length = jnp.where(row8 == i, lens[0, i].astype(F32), length)
+        partner = jnp.where(row8 == i, pair[i].astype(F32), partner)
+    prow[mine] = partner
+    mst[...] = jnp.zeros_like(mst)
+    lst[...] = jnp.ones_like(lst)
+
+    for e in range(NX):
+        k_segment = segment(x_from(e) * TOK + iota((TOK, TOK), 0))
+        bias[e] = jnp.where(k_segment == q_segment, 0.0, -1e30).astype(F32)
+
+    def scores(e, g):
+        key = kb[g, x_from(e)]
+        for j in range(PER):
+            query = qv[:, pl.ds(pl.multiple_of((g * PER + j) * D, D), D)]
+            s = lax.dot_general(key, query, NT, preferred_element_type=F32) * SCALE2 + bias[e]
+            m = jnp.max(s, axis=0, keepdims=True)
+            p = jnp.exp2(s - m)
+            pst[e, g, :, j * TOK : (j + 1) * TOK] = p.astype(BF16)
+            mst[e, g, j : j + 1, :] = m
+            lst[e, g, j : j + 1, :] = jnp.sum(p, axis=0, keepdims=True)
+
     for k in range(1, PLANE):
         p_copies[k] = copy(prow.at[mine], prow.at[mine], p_s.at[k], p_r.at[k], at_plane(k))
         p_copies[k].start()
@@ -173,6 +175,9 @@
         return carry
 
     lax.fori_loop(0, GROUPS, own, 0)
+    pl.semaphore_wait(heard.at[0], 2)
+    for o in (4, -4):
+        pl.semaphore_signal(heard.at[1], inc=1, device_id=at_z(o), device_id_type=MESH)
 
     row16 = lax.rem(iota((2 * DOCS, TOK), 0), DOCS)
 
@@ -189,15 +194,33 @@
             acc = lax.dot_general(lhs, pst[e, g], NT, preferred_element_type=F32)
             wo[g, :, pl.ds(pl.multiple_of(x_from(e) * TOK, TOK), TOK)] = acc[:DOCS] + acc[DOCS:]
 
-    for i in range(GROUPS):
+    def key_copy(d, i):
+        g = lax.rem(x + d + 1 + i, GROUPS)
+        return copy(kb.at[g, x], kb.at[g, x], k_s.at[d, i], k_r.at[d, i], at_x(d))
+
+    def step(i, carry):
         group = lax.rem(x + 1 + i, GROUPS)
-        for d in (1, 3, 2):
-            k_copies[d, i].wait_recv()
+
+        def piece(t, inner):
+            d = 1 + lax.rem(2 * t, NX - 1)
+            key_copy(d, i).wait_recv()
             scores(d, group)
+            return inner
+
+        lax.fori_loop(0, NX - 1, piece, 0)
         weigh(group)
-        if i < GROUPS - 1:
-            w_copies[i + 1] = copy(wo.at[group], wi.at[x], w_s.at[i + 1], w_r.at[i + 1], at_x(i + 1))
-            w_copies[i + 1].start()
+
+        @pl.when(i < GROUPS - 1)
+        def _():
+            copy(wo.at[group], wi.at[x], w_s.at[i + 1], w_r.at[i + 1], at_x(i + 1)).start()
+
+        return carry
+
+    lax.fori_loop(0, GROUPS, step, 0)
+    pl.semaphore_wait(heard.at[1], 2)
+    for d in range(1, NX):
+        group = lax.rem(x + d, GROUPS)
+        w_copies[d] = copy(wo.at[group], wi.at[x], w_s.at[d], w_r.at[d], at_x(d))
     onehot = (segment(iota((DOCS, WIN), 1)) == iota((DOCS, WIN), 0)).astype(F32)
     for d in (1, 3, 2):
         v_copies[d].wait_recv()
@@ -222,7 +245,7 @@
         c_copies[offset] = copy(ucol.at[origin], ucol.at[origin], c_s.at[offset % NZ], c_r.at[offset % NZ], at_z(step))
         c_copies[offset].start()
 
-    for o in FAR + NEAR:
+    for o in FAR + (8,) + NEAR:
         send_col(z, o, o)
     for k in range(1, PLANE):
         u_copies[k] = copy(urow.at[mine], urow.at[mine], u_s.at[k], u_r.at[k], at_plane(k))
@@ -242,15 +265,14 @@
 
     def squares(a):
         wide = a.astype(F32)
-        hi, lo = split2(wide * wide)
-        ones = jnp.ones((2 * DOCS, FEAT), BF16)
-        return (
-            lax.dot_general(ones, hi, NT, preferred_element_type=F32)
-            + lax.dot_general(ones, lo, NT, preferred_element_type=F32)
-        )[:DOCS]
+        return jnp.sum(wide * wide, axis=1, keepdims=True)
+
+    def to_row(column):
+        n = column.shape[0]
+        return jnp.sum(jnp.where(iota((n, D), 0) == iota((n, D), 1), column, 0.0), axis=0, keepdims=True)
 
     dsend[:ROWS, :] = lax.dot_general(rows, cols, NT, preferred_element_type=F32)
-    dsend[ROWS:, :] = jnp.where(row8 == 0, squares(cols), squares(jnp.concatenate([rows, rows], axis=0)))
+    dsend[ROWS:, :] = jnp.where(row8 == 0, to_row(squares(cols)), to_row(squares(rows)))
     d_copies = {d: copy(dsend, drecv.at[x], d_s.at[d], d_r.at[d], at_x(d)) for d in (2, 1, 3)}
     for d in d_copies:
         d_copies[d].start()
@@ -275,7 +297,7 @@
     same = (r_plane == mine) & (c_z == z) & (r_doc == c_doc)
     weight = jnp.where(same, 0.0, jnp.exp(logits))
     col_sum = jnp.sum(weight, axis=0, keepdims=True)
-    row_sum = jnp.sum(jnp.where(eye, jnp.sum(weight, axis=1, keepdims=True), 0.0), axis=0, keepdims=True)
+    row_sum = to_row(jnp.sum(weight, axis=1, keepdims=True))
     ssend[...] = jnp.broadcast_to(col_sum, (DOCS, D))
     rsend[...] = jnp.broadcast_to(row_sum, (DOCS, D))
     t_copies = {}
@@ -290,7 +312,7 @@
     own_radius = norms[pl.ds(pl.multiple_of(mine * DOCS, DOCS), DOCS), :]
     for j in range(PER):
         at = slice(j * D, (j + 1) * D)
-        out[:, at] = (pooled[:, at] / own_radius).astype(BF16).astype(F32)
+        out[:, at] = pooled[:, at] / own_radius
     partners = prow_wait(p_copies, prow).reshape(ROWS, D)
     column_doc = ((y * NZ + c_z) * NC + c) * DOCS + c_doc
     pairs = jnp.where(partners == column_doc.astype(F32), 2.0, 0.0)
@@ -327,8 +349,8 @@
     tail = gradient[:, FEAT:]
     projection = tail[:, :1] + tail[:, D // 2 : D // 2 + 1]
     for j in range(PER):
-        at = slice(j * D, (j + 1) * D)
-        out[:, FEAT + j * D : FEAT + (j + 1) * D] = (gradient[:, at] - out[:, at] * projection) / own_radius
+        out[:, FEAT + j * D : FEAT + (j + 1) * D] = gradient[:, j * D : (j + 1) * D] / own_radius
+    out[:, 2 * FEAT :] = projection / own_radius
 
     for copies in (
         k_copies, v_copies, p_copies, w_copies, c_copies, u_copies, d_copies, t_copies, a_copies, g_copies
@@ -349,7 +371,7 @@
     hbm = pl.BlockSpec(memory_space=pl.ANY)
     both = pl.pallas_call(
         kernel,
-        out_shape=jax.ShapeDtypeStruct((DOCS, 2 * FEAT), F32),
+        out_shape=jax.ShapeDtypeStruct((DOCS, 2 * FEAT + D), F32),
         in_specs=[hbm] * 5,
         out_specs=vmem,
         scratch_shapes=[
@@ -377,6 +399,7 @@
             pltpu.VMEM((PLANE, DOCS, FEAT + D), BF16),
             pltpu.VMEM((PLANE, DOCS, FEAT + D), BF16),
             pltpu.VMEM((ROWS, D), F32),
+            pltpu.SemaphoreType.REGULAR((2,)),
             dma((4 + GROUPS,)),
             dma((NX, GROUPS)), dma((NX, GROUPS)),
             dma((NX,)), dma((NX,)),
@@ -393,7 +416,9 @@
             collective_id=0, has_side_effects=True, vmem_limit_bytes=60 << 20
         ),
     )(document_lengths, pair_ids, queries, keys, values)
-    return both[:, :FEAT].astype(BF16), both[:, FEAT:]
+    embeddings = both[:, :FEAT].astype(BF16)
+    grads = both[:, FEAT : 2 * FEAT] - embeddings.astype(F32) * both[:, 2 * FEAT : 2 * FEAT + 1]
+    return embeddings, grads
 
 
 def solution(mesh):

time: 61.8 us -> 57.2 us (0.926)
  Pallas kernels: 58.2 us -> 54.1 us
  local copies, waits for them, and re-layouts: 2.71 us -> 0.79 us
  other arithmetic: 0 us -> 1.45 us
    pallas_call x1, Pallas kernels: 58.2 us -> 54.1 us  [per_device(): pl.pallas_call(kernel, out_shape=jax.ShapeDtypeStruct((DOCS, 2 * FEAT + D...]
    slice x2 -> x1, local copies, waits for them, and re-layouts: 2.71 us -> 0.79 us  [per_device(): both[:, 2 * FEAT:2 * FEAT + 1]]
    sub x0 -> x1, other arithmetic: none -> 1.45 us  [per_device(): both[:, FEAT:2 * FEAT]]
where the time goes in v3:
time: 57.2 us; the launch traced here: 57 us
  Pallas kernels  54.1 us (95%)
  other arithmetic  1.45 us (3%)
  local copies, waits for them, and re-layouts  0.79 us (1%)
  between operations  0.64 us (1%)
    pallas_call x1, Pallas kernels, per_device(): pl.pallas_call(kernel, out_shape=jax.ShapeDtypeStruct((DOCS, 2 * FEAT + D...  54.1 us
    sub x1, other arithmetic, per_device(): both[:, FEAT:2 * FEAT]  1.45 us

profile of v3, /device:TPU:1, one launch (start us, length us, event | category | flops | bytes accessed | tf_op | source)
XLA Modules:
  0.0 57.0 jit_solution(14714006909379673419)
XLA Ops:
  0.6 54.1 %shard_map.68 = f32[8,1920]{1,0:T(8,128)} custom-call(s32[1,8]{1,0:T(1,128)} %lens_hbm.1, s32[8]{0:T(128)} %pair_hbm.1, bf16[128,3584]{1,0:T(8,128)(2,1)} %q_hbm.1, bf16[128,512]{1,0:T(8,128)(2,1)} %k_hbm.1, bf16[128,512]{1,0:T(8,128)(2,1)} %v_hbm.1), custom_call_target="tpu_custom_call" | custom-call | tf_op jit(solution)/shard_map/pallas_call | solution.py:372
  54.8 0.8 %slice_reduce_fusion = f32[8]{0:T(128)S(1)} fusion(f32[8,1920]{1,0:T(8,128)} %shard_map.68), kind=kLoop, calls=%fused_computation.2 | loop fusion | bytes 64 | tf_op jit(solution)/shard_map/slice | solution.py:420
  55.5 1.4 %multiply_subtract_fusion = (f32[8,896]{1,0:T(8,128)}, bf16[8,896]{1,0:T(8,128)(2,1)}) fusion(f32[8,1920]{1,0:T(8,128)} %shard_map.68, f32[8]{0:T(128)S(1)} %slice_reduce_fusion), kind=kLoop, calls=%fused_computation.1 | loop fusion | flops 21504 | bytes 86048 | tf_op jit(solution)/shard_map/sub | solution.py:420

commit v4 on v3

--- a/solution.py
+++ b/solution.py
@@ -78,20 +78,23 @@
             src_ref=src, dst_ref=dst, send_sem=ss, recv_sem=rs, device_id=there, device_id_type=MESH
         )
 
+    near = [at_plane(1), at_plane(NC), at_plane((NY - 1) * NC), at_z(1), at_z(-1)]
     barrier = pltpu.get_barrier_semaphore()
-    for d in range(1, NX):
+    for d in (2, 1, 3):
         pl.semaphore_signal(barrier, inc=1, device_id=at_x(d), device_id_type=MESH)
-    for k in range(1, PLANE):
-        pl.semaphore_signal(barrier, inc=1, device_id=at_plane(k), device_id_type=MESH)
-    for o in NEAR:
-        pl.semaphore_signal(barrier, inc=1, device_id=at_z(o), device_id_type=MESH)
+    for there in near:
+        pl.semaphore_signal(barrier, inc=1, device_id=there, device_id_type=MESH)
+
+    def tell(level, others):
+        for there in others:
+            pl.semaphore_signal(heard.at[level], inc=1, device_id=there, device_id_type=MESH)
 
     lens_in = pltpu.make_async_copy(lens_hbm, lens, lsem.at[0])
     pair_in = pltpu.make_async_copy(pair_hbm, pair, lsem.at[1])
     q_in = pltpu.make_async_copy(q_hbm, qv, lsem.at[2])
     v_in = pltpu.make_async_copy(v_hbm.at[:, pl.ds(pl.multiple_of(x * D, D), D)], vb.at[x], lsem.at[3])
     k_in = [
-        pltpu.make_async_copy(k_hbm.at[:, g * D : (g + 1) * D], kb.at[g, x], lsem.at[4 + g]) for g in range(GROUPS)
+        pltpu.make_async_copy(k_hbm.at[:, g * D : (g + 1) * D], kb.at[g, 0], lsem.at[4 + g]) for g in range(GROUPS)
     ]
     for one in k_in:
         one.start()
@@ -101,7 +104,7 @@
     v_in.start()
     for one in k_in:
         one.wait()
-    pl.semaphore_wait(barrier, NX - 1 + PLANE - 1 + len(NEAR))
+    pl.semaphore_wait(barrier, NX - 1 + len(near))
 
     k_copies = {}
     v_copies = {}
@@ -110,7 +113,7 @@
     for i in range(GROUPS):
         for d in (1, 3, 2):
             g = lax.rem(x + d + 1 + i, GROUPS)
-            k_copies[d, i] = copy(kb.at[g, x], kb.at[g, x], k_s.at[d, i], k_r.at[d, i], at_x(d))
+            k_copies[d, i] = copy(kb.at[g, 0], kb.at[g, d], k_s.at[d, i], k_r.at[d, i], at_x(d))
             k_copies[d, i].start()
     for d in (1, 3, 2):
         there = lax.rem(x + d, NX)
@@ -118,8 +121,7 @@
             v_hbm.at[:, pl.ds(pl.multiple_of(there * D, D), D)], vb.at[x], v_s.at[d], v_r.at[d], at_x(d)
         )
         v_copies[d].start()
-    for o in (2, -2):
-        pl.semaphore_signal(heard.at[0], inc=1, device_id=at_z(o), device_id_type=MESH)
+    tell(0, near)
     lens_in.wait()
     pair_in.wait()
 
@@ -151,22 +153,20 @@
 
     for e in range(NX):
         k_segment = segment(x_from(e) * TOK + iota((TOK, TOK), 0))
-        bias[e] = jnp.where(k_segment == q_segment, 0.0, -1e30).astype(F32)
-
-    def scores(e, g):
-        key = kb[g, x_from(e)]
+        bias[e * TOK : (e + 1) * TOK] = jnp.where(k_segment == q_segment, 0.0, -1e30).astype(F32)
+
+    def scores(part, g):
+        places = slice(0, TOK) if part == 0 else slice(TOK, WIN)
+        key = kb[g, 0] if part == 0 else kb[g, 1:].reshape(WIN - TOK, D)
         for j in range(PER):
             query = qv[:, pl.ds(pl.multiple_of((g * PER + j) * D, D), D)]
-            s = lax.dot_general(key, query, NT, preferred_element_type=F32) * SCALE2 + bias[e]
+            s = lax.dot_general(key, query, NT, preferred_element_type=F32) * SCALE2 + bias[places]
             m = jnp.max(s, axis=0, keepdims=True)
             p = jnp.exp2(s - m)
-            pst[e, g, :, j * TOK : (j + 1) * TOK] = p.astype(BF16)
-            mst[e, g, j : j + 1, :] = m
-            lst[e, g, j : j + 1, :] = jnp.sum(p, axis=0, keepdims=True)
-
-    for k in range(1, PLANE):
-        p_copies[k] = copy(prow.at[mine], prow.at[mine], p_s.at[k], p_r.at[k], at_plane(k))
-        p_copies[k].start()
+            pst[g, places, j * TOK : (j + 1) * TOK] = p.astype(BF16)
+            mst[part, g, j : j + 1, :] = m
+            lst[part, g, j : j + 1, :] = jnp.sum(p, axis=0, keepdims=True)
+
     q_in.wait()
     v_in.wait()
 
@@ -175,52 +175,58 @@
         return carry
 
     lax.fori_loop(0, GROUPS, own, 0)
-    pl.semaphore_wait(heard.at[0], 2)
-    for o in (4, -4):
-        pl.semaphore_signal(heard.at[1], inc=1, device_id=at_z(o), device_id_type=MESH)
+    pl.semaphore_wait(heard.at[0], len(near))
+    tell(1, [at_z(2), at_z(-2), at_plane(NY // 2 * NC)])
 
     row16 = lax.rem(iota((2 * DOCS, TOK), 0), DOCS)
 
     def weigh(g):
-        ms = [mst[e, g] for e in range(NX)]
-        top = functools.reduce(jnp.maximum, ms)
-        fs = [jnp.exp2(m - top) for m in ms]
-        inv = 1.0 / sum(lst[e, g] * fs[e] for e in range(NX))
-        for e in range(NX):
-            f = fs[e] * inv
+        top = jnp.maximum(mst[0, g], mst[1, g])
+        fs = [jnp.exp2(mst[part, g] - top) for part in range(2)]
+        inv = 1.0 / (lst[0, g] * fs[0] + lst[1, g] * fs[1])
+        lhs = []
+        for f in fs:
+            f = f * inv
             hi = f.astype(BF16).astype(F32)
             both = jnp.concatenate([hi, f - hi], axis=0)
-            lhs = jnp.concatenate([jnp.where(row16 == j, both, 0.0).astype(BF16) for j in range(PER)], axis=1)
-            acc = lax.dot_general(lhs, pst[e, g], NT, preferred_element_type=F32)
-            wo[g, :, pl.ds(pl.multiple_of(x_from(e) * TOK, TOK), TOK)] = acc[:DOCS] + acc[DOCS:]
+            lhs.append(jnp.concatenate([jnp.where(row16 == j, both, 0.0).astype(BF16) for j in range(PER)], axis=1))
+        acc = lax.dot_general(jnp.concatenate(lhs, axis=0), pst[g], NT, preferred_element_type=F32)
+        for e in range(NX):
+            at = 0 if e == 0 else 2 * DOCS
+            half = acc[at : at + 2 * DOCS, e * TOK : (e + 1) * TOK]
+            wo[g, :, pl.ds(pl.multiple_of(x_from(e) * TOK, TOK), TOK)] = half[:DOCS] + half[DOCS:]
 
     def key_copy(d, i):
         g = lax.rem(x + d + 1 + i, GROUPS)
-        return copy(kb.at[g, x], kb.at[g, x], k_s.at[d, i], k_r.at[d, i], at_x(d))
+        return copy(kb.at[g, 0], kb.at[g, d], k_s.at[d, i], k_r.at[d, i], at_x(d))
 
     def step(i, carry):
         group = lax.rem(x + 1 + i, GROUPS)
 
-        def piece(t, inner):
-            d = 1 + lax.rem(2 * t, NX - 1)
+        for d in (1, 3, 2):
             key_copy(d, i).wait_recv()
-            scores(d, group)
-            return inner
-
-        lax.fori_loop(0, NX - 1, piece, 0)
+        scores(1, group)
         weigh(group)
 
         @pl.when(i < GROUPS - 1)
         def _():
             copy(wo.at[group], wi.at[x], w_s.at[i + 1], w_r.at[i + 1], at_x(i + 1)).start()
 
+        @pl.when(i == 0)
+        def _():
+            pl.semaphore_wait(heard.at[1], 3)
+            tell(2, [at_z(4), at_z(-4)])
+
         return carry
 
     lax.fori_loop(0, GROUPS, step, 0)
-    pl.semaphore_wait(heard.at[1], 2)
+    pl.semaphore_wait(heard.at[2], 2)
     for d in range(1, NX):
         group = lax.rem(x + d, GROUPS)
         w_copies[d] = copy(wo.at[group], wi.at[x], w_s.at[d], w_r.at[d], at_x(d))
+    for k in range(1, PLANE):
+        p_copies[k] = copy(prow.at[mine], prow.at[mine], p_s.at[k], p_r.at[k], at_plane(k))
+        p_copies[k].start()
     onehot = (segment(iota((DOCS, WIN), 1)) == iota((DOCS, WIN), 0)).astype(F32)
     for d in (1, 3, 2):
         v_copies[d].wait_recv()
@@ -230,10 +236,11 @@
         weights = weights + wi[x_from(d)]
     lhs = jnp.concatenate([weights[j : j + 1] * onehot for j in range(PER)], axis=0)
     hi, lo = split2(lhs)
-    value = vb[...].reshape(WIN, D)
-    sums = jnp.dot(hi, value, preferred_element_type=F32) + jnp.dot(lo, value, preferred_element_type=F32)
+    sums = jnp.dot(jnp.concatenate([hi, lo], axis=0), vb[...].reshape(WIN, D), preferred_element_type=F32)
+    sums = sums[: PER * DOCS] + sums[PER * DOCS :]
+    per_length = 1.0 / length
     for j in range(PER):
-        pooled[:, j * D : (j + 1) * D] = sums[j * DOCS : (j + 1) * DOCS] / length
+        pooled[:, j * D : (j + 1) * D] = sums[j * DOCS : (j + 1) * DOCS] * per_length
     short = pooled[...].astype(BF16)
     ucol[z] = short
     urow[mine] = short
@@ -256,23 +263,23 @@
             send_col(z_from(o), step, o + step)
     for k in range(1, PLANE):
         u_copies[k].wait_recv()
+
+    def squares(a):
+        wide = a.astype(F32)
+        return jnp.sum(wide * wide, axis=1, keepdims=True)
+
+    def to_row(column):
+        n = column.shape[0]
+        return jnp.sum(jnp.where(iota((n, D), 0) == iota((n, D), 1), column, 0.0), axis=0, keepdims=True)
+
+    rows = urow[...].reshape(ROWS, FEAT)
+    dsend[ROWS:, :] = jnp.broadcast_to(to_row(squares(rows)), (DOCS, D))
     for o in c_copies:
         if o not in FAR:
             c_copies[o].wait_recv()
-
-    rows = urow[...].reshape(ROWS, FEAT)
     cols = ucol[...].reshape(COLS, FEAT)
-
-    def squares(a):
-        wide = a.astype(F32)
-        return jnp.sum(wide * wide, axis=1, keepdims=True)
-
-    def to_row(column):
-        n = column.shape[0]
-        return jnp.sum(jnp.where(iota((n, D), 0) == iota((n, D), 1), column, 0.0), axis=0, keepdims=True)
-
     dsend[:ROWS, :] = lax.dot_general(rows, cols, NT, preferred_element_type=F32)
-    dsend[ROWS:, :] = jnp.where(row8 == 0, to_row(squares(cols)), to_row(squares(rows)))
+    dsend[ROWS : ROWS + 1, :] = to_row(squares(cols))
     d_copies = {d: copy(dsend, drecv.at[x], d_s.at[d], d_r.at[d], at_x(d)) for d in (2, 1, 3)}
     for d in d_copies:
         d_copies[d].start()
@@ -288,81 +295,67 @@
     def to_column(row):
         return jnp.sum(jnp.where(eye, row, 0.0), axis=1, keepdims=True)
 
-    radius = jnp.sqrt(to_column(full[ROWS + 1 : ROWS + 2]) + 1e-6)
-    norms[...] = jnp.broadcast_to(radius, (ROWS, D))
-    inv_cols = 1.0 / jnp.sqrt(full[ROWS : ROWS + 1] + 1e-6)
-    logits = full[:ROWS] * ((1.0 / radius) * (inv_cols * INV_TEMP))
+    inv_rows = 1.0 / jnp.sqrt(to_column(full[ROWS + 1 : ROWS + 2]) + 1e-6)
+    inv_cols = INV_TEMP / jnp.sqrt(full[ROWS : ROWS + 1] + 1e-6)
+    logits = full[:ROWS] * (inv_rows * inv_cols)
     r_plane, r_doc = r_id // DOCS, lax.rem(r_id, DOCS)
     c_z, c_doc = c_id // DOCS, lax.rem(c_id, DOCS)
     same = (r_plane == mine) & (c_z == z) & (r_doc == c_doc)
     weight = jnp.where(same, 0.0, jnp.exp(logits))
     col_sum = jnp.sum(weight, axis=0, keepdims=True)
-    row_sum = to_row(jnp.sum(weight, axis=1, keepdims=True))
     ssend[...] = jnp.broadcast_to(col_sum, (DOCS, D))
-    rsend[...] = jnp.broadcast_to(row_sum, (DOCS, D))
     t_copies = {}
     a_copies = {}
     for o in (8, 7, -7, 6, -6, 5, -5, 4, -4, 3, -3, 2, -2, 1, -1):
         t_copies[o] = copy(ssend.at[pl.ds(0, 1)], scol.at[z, pl.ds(0, 1)], t_s.at[o % NZ], t_r.at[o % NZ], at_z(o))
         t_copies[o].start()
+    row_sum = to_row(jnp.sum(weight, axis=1, keepdims=True))
+    rsend[...] = jnp.broadcast_to(row_sum, (DOCS, D))
     for k in range(1, PLANE):
         a_copies[k] = copy(rsend.at[pl.ds(0, 1)], srow.at[mine, pl.ds(0, 1)], a_s.at[k], a_r.at[k], at_plane(k))
         a_copies[k].start()
 
-    own_radius = norms[pl.ds(pl.multiple_of(mine * DOCS, DOCS), DOCS), :]
+    norms[...] = jnp.broadcast_to(inv_rows, (ROWS, D))
+    own_inverse = norms[pl.ds(pl.multiple_of(mine * DOCS, DOCS), DOCS), :]
     for j in range(PER):
         at = slice(j * D, (j + 1) * D)
-        out[:, at] = pooled[:, at] / own_radius
-    partners = prow_wait(p_copies, prow).reshape(ROWS, D)
+        out[:, at] = pooled[:, at] * own_inverse
+    for k in p_copies:
+        p_copies[k].wait_recv()
+    partners = prow[...].reshape(ROWS, D)
     column_doc = ((y * NZ + c_z) * NC + c) * DOCS + c_doc
     pairs = jnp.where(partners == column_doc.astype(F32), 2.0, 0.0)
     for k in range(1, PLANE):
         a_copies[k].wait_recv()
         row_sum = row_sum + srow[slot_from(k), 0:1, :]
-    for o in t_copies:
+    scale = inv_rows * inv_cols
+    ready = (weight * (1.0 / to_column(row_sum)) - pairs) * scale
+    scaled_weight = weight * scale
+    undone = full[:ROWS] * inv_rows
+    for o in reversed(list(t_copies)):
         t_copies[o].wait_recv()
         col_sum = col_sum + scol[z_from(o), 0:1, :]
-    coef = weight * (1.0 / to_column(row_sum) + 1.0 / col_sum) - pairs
-    along = jnp.sum(coef * logits, axis=1, keepdims=True)
-    scaled = coef * (inv_cols * INV_TEMP)
-    hi = scaled.astype(BF16)
-    rest = scaled - hi.astype(F32)
-    mid, lo = split2(rest)
-    piece = (
-        jnp.dot(hi, cols, preferred_element_type=F32)
-        + jnp.dot(mid, cols, preferred_element_type=F32)
-        + jnp.dot(lo, cols, preferred_element_type=F32)
-    )
-    high, low = split2(along)
-    first = iota((ROWS, D), 1) < D // 2
-    sides = jnp.where(first, high.astype(F32), low.astype(F32)).astype(BF16)
-    gsend[:, :, :FEAT] = piece.astype(BF16).reshape(PLANE, DOCS, FEAT)
-    gsend[:, :, FEAT:] = sides.reshape(PLANE, DOCS, D)
+    scaled = scaled_weight * (1.0 / col_sum) + ready
+    along = jnp.sum(scaled * undone, axis=1, keepdims=True)
+    hi, lo = split2(scaled)
+    parts = jnp.dot(jnp.concatenate([hi, lo], axis=0), cols, preferred_element_type=F32)
+    gsend[:, :, :FEAT] = (parts[:ROWS] + parts[ROWS:]).astype(BF16).reshape(PLANE, DOCS, FEAT)
+    gsend[:, :, FEAT:] = jnp.broadcast_to(along, (ROWS, D)).astype(BF16).reshape(PLANE, DOCS, D)
     g_copies = {}
-    for k in range(PLANE - 1, 0, -1):
+    for k in (5, 4, 7, 3, 6, 2, 1):
         g_copies[k] = copy(gsend.at[slot_to(k)], grecv.at[mine], g_s.at[k], g_r.at[k], at_plane(k))
         g_copies[k].start()
     gradient = gsend[mine].astype(F32)
     for k in range(1, PLANE):
         g_copies[k].wait_recv()
         gradient = gradient + grecv[slot_from(k)].astype(F32)
-    tail = gradient[:, FEAT:]
-    projection = tail[:, :1] + tail[:, D // 2 : D // 2 + 1]
-    for j in range(PER):
-        out[:, FEAT + j * D : FEAT + (j + 1) * D] = gradient[:, j * D : (j + 1) * D] / own_radius
-    out[:, 2 * FEAT :] = projection / own_radius
+    out[:, FEAT:] = gradient
 
     for copies in (
         k_copies, v_copies, p_copies, w_copies, c_copies, u_copies, d_copies, t_copies, a_copies, g_copies
     ):
         for key in copies:
             copies[key].wait_send()
-
-
-def prow_wait(p_copies, prow):
-    for k in p_copies:
-        p_copies[k].wait_recv()
-    return prow[...]
 
 
 def per_device(queries, keys, values, document_lengths, pair_ids):
@@ -380,10 +373,10 @@
             pltpu.VMEM((TOK, HEADS * D), BF16),
             pltpu.VMEM((GROUPS, NX, TOK, D), BF16),
             pltpu.VMEM((NX, TOK, D), BF16),
-            pltpu.VMEM((NX, TOK, TOK), F32),
-            pltpu.VMEM((NX, GROUPS, TOK, PER * TOK), BF16),
-            pltpu.VMEM((NX, GROUPS, DOCS, TOK), F32),
-            pltpu.VMEM((NX, GROUPS, DOCS, TOK), F32),
+            pltpu.VMEM((WIN, TOK), F32),
+            pltpu.VMEM((GROUPS, WIN, PER * TOK), BF16),
+            pltpu.VMEM((2, GROUPS, DOCS, TOK), F32),
+            pltpu.VMEM((2, GROUPS, DOCS, TOK), F32),
             pltpu.VMEM((GROUPS, DOCS, WIN), F32),
             pltpu.VMEM((NX, DOCS, WIN), F32),
             pltpu.VMEM((DOCS, FEAT), F32),
@@ -399,7 +392,7 @@
             pltpu.VMEM((PLANE, DOCS, FEAT + D), BF16),
             pltpu.VMEM((PLANE, DOCS, FEAT + D), BF16),
             pltpu.VMEM((ROWS, D), F32),
-            pltpu.SemaphoreType.REGULAR((2,)),
+            pltpu.SemaphoreType.REGULAR((3,)),
             dma((4 + GROUPS,)),
             dma((NX, GROUPS)), dma((NX, GROUPS)),
             dma((NX,)), dma((NX,)),

time: 57.2 us -> 56.5 us (0.988)
  Pallas kernels: 54.1 us -> 53.4 us
    pallas_call x1, Pallas kernels: 54.1 us -> 53.4 us  [per_device(): pl.pallas_call(kernel, out_shape=jax.ShapeDtypeStruct((DOCS, 2 * FEAT + D...]
where the time goes in v4:
time: 56.5 us; the launch traced here: 56.3 us
  Pallas kernels  53.4 us (95%)
  other arithmetic  1.45 us (3%)
  local copies, waits for them, and re-layouts  0.79 us (1%)
  between operations  0.64 us (1%)
    pallas_call x1, Pallas kernels, per_device(): pl.pallas_call(kernel, out_shape=jax.ShapeDtypeStruct((DOCS, 2 * FEAT + D...  53.4 us
    sub x1, other arithmetic, per_device(): both[:, FEAT:2 * FEAT]  1.45 us

profile of v4, /device:TPU:1, one launch (start us, length us, event | category | flops | bytes accessed | tf_op | source)
XLA Modules:
  0.0 56.3 jit_solution(16803520037117521322)
XLA Ops:
  0.6 53.4 %shard_map.68 = f32[8,1920]{1,0:T(8,128)} custom-call(s32[1,8]{1,0:T(1,128)} %lens_hbm.1, s32[8]{0:T(128)} %pair_hbm.1, bf16[128,3584]{1,0:T(8,128)(2,1)} %q_hbm.1, bf16[128,512]{1,0:T(8,128)(2,1)} %k_hbm.1, bf16[128,512]{1,0:T(8,128)(2,1)} %v_hbm.1), custom_call_target="tpu_custom_call" | custom-call | tf_op jit(solution)/shard_map/pallas_call | solution.py:365
  54.0 0.8 %slice_reduce_fusion = f32[8]{0:T(128)S(1)} fusion(f32[8,1920]{1,0:T(8,128)} %shard_map.68), kind=kLoop, calls=%fused_computation.2 | loop fusion | bytes 64 | tf_op jit(solution)/shard_map/slice | solution.py:413
  54.8 1.4 %multiply_subtract_fusion = (f32[8,896]{1,0:T(8,128)}, bf16[8,896]{1,0:T(8,128)(2,1)}) fusion(f32[8,1920]{1,0:T(8,128)} %shard_map.68, f32[8]{0:T(128)S(1)} %slice_reduce_fusion), kind=kLoop, calls=%fused_computation.1 | loop fusion | flops 21504 | bytes 86048 | tf_op jit(solution)/shard_map/sub | solution.py:413

commit v5 on v4

--- a/solution.py
+++ b/solution.py
@@ -28,9 +28,9 @@
 INV_TEMP = 50.0
 SCALE2 = D ** (-0.5) * math.log2(math.e)
 
-NEAR = (1, -1, 2, -2)
-FAR = (5, -5)
-FORWARD = {5: (2, -2, 1, -1), -5: (-2, 2, -1, 1)}
+NEAR = ()
+FAR = (1, -1, 5, -5)
+FORWARD = {1: (1,), -1: (-1,), 5: (1, -2, -1), -5: (-1, 2, 1)}
 
 
 def split2(a):
@@ -39,10 +39,10 @@
 
 
 def kernel(
-    lens_hbm, pair_hbm, q_hbm, k_hbm, v_hbm, out,
+    lens_hbm, pair_hbm, q_hbm, k_hbm, v_hbm, out_hbm,
     lens, pair, qv, kb, vb, bias, pst, mst, lst, wo, wi, pooled, ucol, urow, prow,
-    dsend, drecv, ssend, scol, rsend, srow, gsend, grecv, norms,
-    heard, lsem, k_s, k_r, v_s, v_r, w_s, w_r, p_s, p_r, u_s, u_r, c_s, c_r, d_s, d_r, t_s, t_r, a_s, a_r, g_s, g_r,
+    dsend, drecv, ssend, scol, rsend, srow, gsend, grecv, norms, out,
+    heard, osem, lsem, k_s, k_r, v_s, v_r, w_s, w_r, p_s, p_r, u_s, u_r, c_s, c_r, d_s, d_r, t_s, t_r, a_s, a_r, g_s, g_r,
 ):
     dp = lax.axis_index("dp")
     x = lax.axis_index("sp")
@@ -252,7 +252,7 @@
         c_copies[offset] = copy(ucol.at[origin], ucol.at[origin], c_s.at[offset % NZ], c_r.at[offset % NZ], at_z(step))
         c_copies[offset].start()
 
-    for o in FAR + (8,) + NEAR:
+    for o in (5, -5, 7, -7, 8, 1, -1):
         send_col(z, o, o)
     for k in range(1, PLANE):
         u_copies[k] = copy(urow.at[mine], urow.at[mine], u_s.at[k], u_r.at[k], at_plane(k))
@@ -320,6 +320,8 @@
     for j in range(PER):
         at = slice(j * D, (j + 1) * D)
         out[:, at] = pooled[:, at] * own_inverse
+    emb_out = pltpu.make_async_copy(out.at[:, pl.ds(0, FEAT)], out_hbm.at[:, pl.ds(0, FEAT)], osem.at[0])
+    emb_out.start()
     for k in p_copies:
         p_copies[k].wait_recv()
     partners = prow[...].reshape(ROWS, D)
@@ -350,23 +352,26 @@
         g_copies[k].wait_recv()
         gradient = gradient + grecv[slot_from(k)].astype(F32)
     out[:, FEAT:] = gradient
+    grad_out = pltpu.make_async_copy(out.at[:, pl.ds(FEAT, FEAT + D)], out_hbm.at[:, pl.ds(FEAT, FEAT + D)], osem.at[1])
+    grad_out.start()
 
     for copies in (
         k_copies, v_copies, p_copies, w_copies, c_copies, u_copies, d_copies, t_copies, a_copies, g_copies
     ):
         for key in copies:
             copies[key].wait_send()
+    emb_out.wait()
+    grad_out.wait()
 
 
 def per_device(queries, keys, values, document_lengths, pair_ids):
     dma = pltpu.SemaphoreType.DMA
-    vmem = pl.BlockSpec(memory_space=pltpu.VMEM)
     hbm = pl.BlockSpec(memory_space=pl.ANY)
     both = pl.pallas_call(
         kernel,
         out_shape=jax.ShapeDtypeStruct((DOCS, 2 * FEAT + D), F32),
         in_specs=[hbm] * 5,
-        out_specs=vmem,
+        out_specs=hbm,
         scratch_shapes=[
             pltpu.SMEM((1, DOCS), jnp.int32),
             pltpu.SMEM((DOCS,), jnp.int32),
@@ -392,7 +397,9 @@
             pltpu.VMEM((PLANE, DOCS, FEAT + D), BF16),
             pltpu.VMEM((PLANE, DOCS, FEAT + D), BF16),
             pltpu.VMEM((ROWS, D), F32),
+            pltpu.VMEM((DOCS, 2 * FEAT + D), F32),
             pltpu.SemaphoreType.REGULAR((3,)),
+            dma((2,)),
             dma((4 + GROUPS,)),
             dma((NX, GROUPS)), dma((NX, GROUPS)),
             dma((NX,)), dma((NX,)),

time: 56.5 us -> 56.1 us (level)
  no operation moved by 1% of the time
where the time goes in v5:
time: 56.1 us; the launch traced here: 55.9 us
  Pallas kernels  53 us (94%)
  other arithmetic  1.45 us (3%)
  local copies, waits for them, and re-layouts  0.79 us (1%)
  between operations  0.64 us (1%)
    pallas_call x1, Pallas kernels, per_device(): pl.pallas_call(kernel, out_shape=jax.ShapeDtypeStruct((DOCS, 2 * FEAT + D...  53 us
    sub x1, other arithmetic, per_device(): both[:, FEAT:2 * FEAT]  1.45 us

profile of v5, /device:TPU:1, one launch (start us, length us, event | category | flops | bytes accessed | tf_op | source)
XLA Modules:
  0.0 55.9 jit_solution(1973924741142511311)
XLA Ops:
  0.6 53.0 %shard_map.68 = f32[8,1920]{1,0:T(8,128)} custom-call(s32[1,8]{1,0:T(1,128)} %lens_hbm.1, s32[8]{0:T(128)} %pair_hbm.1, bf16[128,3584]{1,0:T(8,128)(2,1)} %q_hbm.1, bf16[128,512]{1,0:T(8,128)(2,1)} %k_hbm.1, bf16[128,512]{1,0:T(8,128)(2,1)} %v_hbm.1), custom_call_target="tpu_custom_call" | custom-call | tf_op jit(solution)/shard_map/pallas_call | solution.py:370
  53.7 0.8 %slice_reduce_fusion = f32[8]{0:T(128)S(1)} fusion(f32[8,1920]{1,0:T(8,128)} %shard_map.68), kind=kLoop, calls=%fused_computation.2 | loop fusion | bytes 64 | tf_op jit(solution)/shard_map/slice | solution.py:420
  54.5 1.4 %multiply_subtract_fusion = (f32[8,896]{1,0:T(8,128)}, bf16[8,896]{1,0:T(8,128)(2,1)}) fusion(f32[8,1920]{1,0:T(8,128)} %shard_map.68, f32[8]{0:T(128)S(1)} %slice_reduce_fusion), kind=kLoop, calls=%fused_computation.1 | loop fusion | flops 21504 | bytes 86048 | tf_op jit(solution)/shard_map/sub | solution.py:420

commit v6 on v5

--- a/solution.py
+++ b/solution.py
@@ -341,8 +341,8 @@
     along = jnp.sum(scaled * undone, axis=1, keepdims=True)
     hi, lo = split2(scaled)
     parts = jnp.dot(jnp.concatenate([hi, lo], axis=0), cols, preferred_element_type=F32)
-    gsend[:, :, :FEAT] = (parts[:ROWS] + parts[ROWS:]).astype(BF16).reshape(PLANE, DOCS, FEAT)
-    gsend[:, :, FEAT:] = jnp.broadcast_to(along, (ROWS, D)).astype(BF16).reshape(PLANE, DOCS, D)
+    gsend[:, :, :FEAT] = (parts[:ROWS] + parts[ROWS:]).reshape(PLANE, DOCS, FEAT)
+    gsend[:, :, FEAT:] = jnp.broadcast_to(along, (ROWS, D)).reshape(PLANE, DOCS, D)
     g_copies = {}
     for k in (5, 4, 7, 3, 6, 2, 1):
         g_copies[k] = copy(gsend.at[slot_to(k)], grecv.at[mine], g_s.at[k], g_r.at[k], at_plane(k))
@@ -394,8 +394,8 @@
             pltpu.VMEM((NZ, DOCS, D), F32),
             pltpu.VMEM((DOCS, D), F32),
             pltpu.VMEM((PLANE, DOCS, D), F32),
-            pltpu.VMEM((PLANE, DOCS, FEAT + D), BF16),
-            pltpu.VMEM((PLANE, DOCS, FEAT + D), BF16),
+            pltpu.VMEM((PLANE, DOCS, FEAT + D), F32),
+            pltpu.VMEM((PLANE, DOCS, FEAT + D), F32),
             pltpu.VMEM((ROWS, D), F32),
             pltpu.VMEM((DOCS, 2 * FEAT + D), F32),
             pltpu.SemaphoreType.REGULAR((3,)),

time: 56.1 us -> 56.9 us (1.014)
  Pallas kernels: 53 us -> 53.8 us
    pallas_call x1, Pallas kernels: 53 us -> 53.8 us  [per_device(): pl.pallas_call(kernel, out_shape=jax.ShapeDtypeStruct((DOCS, 2 * FEAT + D...]
where the time goes in v6:
time: 56.9 us; the launch traced here: 56.6 us
  Pallas kernels  53.8 us (95%)
  other arithmetic  1.45 us (3%)
  local copies, waits for them, and re-layouts  0.79 us (1%)
  between operations  0.64 us (1%)
    pallas_call x1, Pallas kernels, per_device(): pl.pallas_call(kernel, out_shape=jax.ShapeDtypeStruct((DOCS, 2 * FEAT + D...  53.8 us
    sub x1, other arithmetic, per_device(): both[:, FEAT:2 * FEAT]  1.45 us

profile of v6, /device:TPU:1, one launch (start us, length us, event | category | flops | bytes accessed | tf_op | source)
XLA Modules:
  0.0 56.6 jit_solution(1266865044379919874)
XLA Ops:
  0.6 53.8 %shard_map.68 = f32[8,1920]{1,0:T(8,128)} custom-call(s32[1,8]{1,0:T(1,128)} %lens_hbm.1, s32[8]{0:T(128)} %pair_hbm.1, bf16[128,3584]{1,0:T(8,128)(2,1)} %q_hbm.1, bf16[128,512]{1,0:T(8,128)(2,1)} %k_hbm.1, bf16[128,512]{1,0:T(8,128)(2,1)} %v_hbm.1), custom_call_target="tpu_custom_call" | custom-call | tf_op jit(solution)/shard_map/pallas_call | solution.py:370
  54.4 0.8 %slice_reduce_fusion = f32[8]{0:T(128)S(1)} fusion(f32[8,1920]{1,0:T(8,128)} %shard_map.68), kind=kLoop, calls=%fused_computation.2 | loop fusion | bytes 64 | tf_op jit(solution)/shard_map/slice | solution.py:420
  55.2 1.4 %multiply_subtract_fusion = (f32[8,896]{1,0:T(8,128)}, bf16[8,896]{1,0:T(8,128)(2,1)}) fusion(f32[8,1920]{1,0:T(8,128)} %shard_map.68, f32[8]{0:T(128)S(1)} %slice_reduce_fusion), kind=kLoop, calls=%fused_computation.1 | loop fusion | flops 21504 | bytes 86048 | tf_op jit(solution)/shard_map/sub | solution.py:420

commit v7 on v5

--- a/solution.py
+++ b/solution.py
@@ -342,7 +342,9 @@
     hi, lo = split2(scaled)
     parts = jnp.dot(jnp.concatenate([hi, lo], axis=0), cols, preferred_element_type=F32)
     gsend[:, :, :FEAT] = (parts[:ROWS] + parts[ROWS:]).astype(BF16).reshape(PLANE, DOCS, FEAT)
-    gsend[:, :, FEAT:] = jnp.broadcast_to(along, (ROWS, D)).astype(BF16).reshape(PLANE, DOCS, D)
+    high, low = split2(along)
+    sides = jnp.where(c_id < D // 2, high.astype(F32), low.astype(F32))
+    gsend[:, :, FEAT:] = sides.astype(BF16).reshape(PLANE, DOCS, D)
     g_copies = {}
     for k in (5, 4, 7, 3, 6, 2, 1):
         g_copies[k] = copy(gsend.at[slot_to(k)], grecv.at[mine], g_s.at[k], g_r.at[k], at_plane(k))
@@ -417,7 +419,8 @@
         ),
     )(document_lengths, pair_ids, queries, keys, values)
     embeddings = both[:, :FEAT].astype(BF16)
-    grads = both[:, FEAT : 2 * FEAT] - embeddings.astype(F32) * both[:, 2 * FEAT : 2 * FEAT + 1]
+    side = both[:, 2 * FEAT :]
+    grads = both[:, FEAT : 2 * FEAT] - embeddings.astype(F32) * (side[:, :1] + side[:, D // 2 : D // 2 + 1])
     return embeddings, grads
 
 

time: 56.1 us -> 56.3 us (level)
  other arithmetic: 1.45 us -> 2.38 us
  local copies, waits for them, and re-layouts: 0.79 us -> 0 us
    add x0 -> x1, other arithmetic: none -> 0.93 us  [per_device(): side[:, :1] + side[:, D // 2:D // 2 + 1]]
    slice x1 -> x0, local copies, waits for them, and re-layouts: 0.79 us -> none  [per_device(): both[:, 2 * FEAT:2 * FEAT + 1]]
where the time goes in v7:
time: 56.3 us; the launch traced here: 56.1 us
  Pallas kernels  53 us (94%)
  other arithmetic  2.38 us (4%)
  between operations  0.64 us (1%)
    pallas_call x1, Pallas kernels, per_device(): pl.pallas_call(kernel, out_shape=jax.ShapeDtypeStruct((DOCS, 2 * FEAT + D...  53 us
    sub x1, other arithmetic, per_device(): both[:, FEAT:2 * FEAT]  1.45 us

profile of v7, /device:TPU:1, one launch (start us, length us, event | category | flops | bytes accessed | tf_op | source)
XLA Modules:
  0.0 56.1 jit_solution(15915357620543584169)
XLA Ops:
  0.6 53.0 %shard_map.68 = f32[8,1920]{1,0:T(8,128)} custom-call(s32[1,8]{1,0:T(1,128)} %lens_hbm.1, s32[8]{0:T(128)} %pair_hbm.1, bf16[128,3584]{1,0:T(8,128)(2,1)} %q_hbm.1, bf16[128,512]{1,0:T(8,128)(2,1)} %k_hbm.1, bf16[128,512]{1,0:T(8,128)(2,1)} %v_hbm.1), custom_call_target="tpu_custom_call" | custom-call | tf_op jit(solution)/shard_map/pallas_call | solution.py:372
  53.7 0.9 %add_reduce_fusion = f32[8]{0:T(128)S(1)} fusion(f32[8,1920]{1,0:T(8,128)} %shard_map.68), kind=kLoop, calls=%fused_computation.2 | loop fusion | flops 8 | bytes 96 | tf_op jit(solution)/shard_map/add | solution.py:423
  54.6 1.4 %multiply_subtract_fusion = (f32[8,896]{1,0:T(8,128)}, bf16[8,896]{1,0:T(8,128)(2,1)}) fusion(f32[8,1920]{1,0:T(8,128)} %shard_map.68, f32[8]{0:T(128)S(1)} %add_reduce_fusion), kind=kLoop, calls=%fused_computation.1 | loop fusion | flops 21504 | bytes 86048 | tf_op jit(solution)/shard_map/sub | solution.py:423

commit v8 on v7

--- a/solution.py
+++ b/solution.py
@@ -353,7 +353,9 @@
     for k in range(1, PLANE):
         g_copies[k].wait_recv()
         gradient = gradient + grecv[slot_from(k)].astype(F32)
-    out[:, FEAT:] = gradient
+    out[:, FEAT : 2 * FEAT] = gradient[:, :FEAT]
+    tail = gradient[:, FEAT:]
+    out[:, 2 * FEAT :] = jnp.broadcast_to(tail[:, :1] + tail[:, D // 2 : D // 2 + 1], (DOCS, D))
     grad_out = pltpu.make_async_copy(out.at[:, pl.ds(FEAT, FEAT + D)], out_hbm.at[:, pl.ds(FEAT, FEAT + D)], osem.at[1])
     grad_out.start()
 
@@ -419,8 +421,7 @@
         ),
     )(document_lengths, pair_ids, queries, keys, values)
     embeddings = both[:, :FEAT].astype(BF16)
-    side = both[:, 2 * FEAT :]
-    grads = both[:, FEAT : 2 * FEAT] - embeddings.astype(F32) * (side[:, :1] + side[:, D // 2 : D // 2 + 1])
+    grads = both[:, FEAT : 2 * FEAT] - embeddings.astype(F32) * both[:, 2 * FEAT : 2 * FEAT + 1]
     return embeddings, grads
 
 

time: 56.3 us -> 56.3 us (level)
  other arithmetic: 2.38 us -> 1.45 us
  local copies, waits for them, and re-layouts: 0 us -> 0.79 us
    add x1 -> x0, other arithmetic: 0.93 us -> none  [per_device(): side[:, :1] + side[:, D // 2:D // 2 + 1]]
    slice x0 -> x1, local copies, waits for them, and re-layouts: none -> 0.79 us  [per_device(): both[:, 2 * FEAT:2 * FEAT + 1]]
where the time goes in v8:
time: 56.3 us; the launch traced here: 56 us
  Pallas kernels  53.2 us (94%)
  other arithmetic  1.45 us (3%)
  local copies, waits for them, and re-layouts  0.79 us (1%)
  between operations  0.64 us (1%)
    pallas_call x1, Pallas kernels, per_device(): pl.pallas_call(kernel, out_shape=jax.ShapeDtypeStruct((DOCS, 2 * FEAT + D...  53.2 us
    sub x1, other arithmetic, per_device(): both[:, FEAT:2 * FEAT]  1.45 us

profile of v8, /device:TPU:1, one launch (start us, length us, event | category | flops | bytes accessed | tf_op | source)
XLA Modules:
  0.0 56.0 jit_solution(4766290010734227960)
XLA Ops:
  0.6 53.2 %shard_map.68 = f32[8,1920]{1,0:T(8,128)} custom-call(s32[1,8]{1,0:T(1,128)} %lens_hbm.1, s32[8]{0:T(128)} %pair_hbm.1, bf16[128,3584]{1,0:T(8,128)(2,1)} %q_hbm.1, bf16[128,512]{1,0:T(8,128)(2,1)} %k_hbm.1, bf16[128,512]{1,0:T(8,128)(2,1)} %v_hbm.1), custom_call_target="tpu_custom_call" | custom-call | tf_op jit(solution)/shard_map/pallas_call | solution.py:374
  53.8 0.8 %slice_reduce_fusion = f32[8]{0:T(128)S(1)} fusion(f32[8,1920]{1,0:T(8,128)} %shard_map.68), kind=kLoop, calls=%fused_computation.2 | loop fusion | bytes 64 | tf_op jit(solution)/shard_map/slice | solution.py:424
  54.6 1.4 %multiply_subtract_fusion = (f32[8,896]{1,0:T(8,128)}, bf16[8,896]{1,0:T(8,128)(2,1)}) fusion(f32[8,1920]{1,0:T(8,128)} %shard_map.68, f32[8]{0:T(128)S(1)} %slice_reduce_fusion), kind=kLoop, calls=%fused_computation.1 | loop fusion | flops 21504 | bytes 86048 | tf_op jit(solution)/shard_map/sub | solution.py:424
